TPU v7x, 128 devices: a whole 4x4x4 slice. The times are simulated.
128 devices in a mesh: prompt: 8 (over x, z_hi), sample: 16 (over y, z_lo, core).
Axes of the slice: x: 4, y: 4, z: 4 (z_hi: 2, z_lo: 2; z = z_hi * 2 + z_lo), core: 2. Of those that a mesh axis runs over, the one named last changes fastest.
Arguments:
- queries: bfloat16 [256, 32, 576], P(('prompt', 'sample')), may hold values from -60 to 60
- new_keys: bfloat16 [256, 576], P(('prompt', 'sample')), may hold values from -60 to 60
- cache: bfloat16 [8, 32768, 576], P('prompt', 'sample'), may hold values from -6 to 6
- residual: bfloat16 [256, 7168], P(('prompt', 'sample')), may hold values from -1.5 to 1.5
- w_uv: bfloat16 [32, 512, 128], replicated, may hold values from -0.25 to 0.25
- w_out: bfloat16 [4096, 7168], P('sample'), may hold values from -0.09375 to 0.09375
- norm_gain: bfloat16 [7168], replicated, may hold values from 0.25 to 1.75
- router: bfloat16 [7168, 16], replicated, may hold values from -0.0625 to 0.0625
- expert_ids: int32 [256, 8], P(('prompt', 'sample')), may hold values from 0 to 15, all different within a row; in each aligned block of 2 rows (0 to 1, 2 to 3, ...) at most 2 rows name the same one
- w_gate: bfloat16 [128, 7168, 256], P(('prompt', 'sample')), may hold values from -0.0625 to 0.0625
- w_up: bfloat16 [128, 7168, 256], P(('prompt', 'sample')), may hold values from -0.0625 to 0.0625
- w_down: bfloat16 [128, 256, 7168], P(('prompt', 'sample')), may hold values from -0.125 to 0.125
- accept: int32 [8, 16], P('prompt', 'sample'), may hold values 0 or 1
- assign: int32 [8, 32], P('prompt'), may hold values from 0 to 31, each once within a row
Outputs:
- trainer_rows: bfloat16 [256, 7168], P(('prompt', 'sample'))
Inputs may be any that keep to these rules, and one draw needn't show every extreme that they name: `expert_ids`: in each device's 2 rows no expert is named more than 2 times, a bound that some block reaches. `assign`: each row is a permutation of 0 to 31.
All inputs are finite; a program needn't handle non-finite values. No bound on the sum of `accept` on one device may be relied on, other than what follows from the above.
Results may differ from a plain program's by a relative error of at most 0.02.
Values may be sent and summed in bfloat16 or wider, within the bound.
A program may use at most 128 MiB of HBM per device.

v0:
```python
import jax
import jax.numpy as jnp
from jax import lax
from jax.sharding import PartitionSpec as P

score_scale = 192.0 ** (-0.5)
route_scale = 2.827
norm_eps = 1e-06


def local(
    queries,
    new_keys,
    cache,
    residual,
    w_uv,
    w_out,
    norm_gain,
    router,
    expert_ids,
    w_gate,
    w_up,
    w_down,
    accept,
    assign,
):
    tok_dev, heads, key_dim = queries.shape
    lat = w_uv.shape[1]
    vdim = w_uv.shape[2]
    groups = lax.axis_size("sample")
    start_row = lax.axis_index("sample") * tok_dev
    zero_index = start_row * 0
    group_tok = tok_dev * groups
    every_query = lax.all_gather(queries, "sample", axis=0, tiled=True)
    keys = cache[0]
    scores = (
        jnp.einsum("ghk,lk->ghl", every_query, keys, preferred_element_type=jnp.float32)
        * score_scale
    )
    own = new_keys.reshape(tok_dev // 2, 2, key_dim)
    own_queries = queries.reshape(tok_dev // 2, 2, heads, key_dim)
    own_scores = (
        jnp.einsum("sthk,suk->sthu", own_queries, own, preferred_element_type=jnp.float32)
        * score_scale
    )
    causal = lax.iota(jnp.int32, 2)[:, None] >= lax.iota(jnp.int32, 2)[None, :]
    causal = causal[None, :, None, :]
    own_peak = jnp.max(jnp.where(causal, own_scores, -jnp.inf), axis=-1).reshape(tok_dev, heads)
    own_peak_full = lax.dynamic_update_slice(
        jnp.full((group_tok, heads), -jnp.inf, jnp.float32), own_peak, (start_row, zero_index)
    )
    local_peak = jnp.maximum(jnp.max(scores, axis=-1), own_peak_full)
    shift = lax.pmax(local_peak, "sample")
    weights = jnp.exp(scores - shift[..., None])
    mine_peak = lax.dynamic_slice(shift, (start_row, zero_index), (tok_dev, heads)).reshape(
        tok_dev // 2, 2, heads
    )
    own_weights = jnp.where(causal, jnp.exp(own_scores - mine_peak[..., None]), 0.0)
    own_denom = jnp.sum(own_weights, axis=-1).reshape(tok_dev, heads)
    denom = jnp.sum(weights, axis=-1) + lax.dynamic_update_slice(
        jnp.zeros((group_tok, heads), jnp.float32), own_denom, (start_row, zero_index)
    )
    latent_sum = jnp.einsum(
        "ghl,lc->ghc",
        weights.astype(jnp.bfloat16),
        keys[:, :lat],
        preferred_element_type=jnp.float32,
    )
    own_latent = jnp.einsum(
        "sthu,suc->sthc",
        own_weights.astype(jnp.bfloat16),
        own[..., :lat],
        preferred_element_type=jnp.float32,
    ).reshape(tok_dev, heads, lat)
    latent_sum = latent_sum + lax.dynamic_update_slice(
        jnp.zeros((group_tok, heads, lat), jnp.float32),
        own_latent,
        (start_row, zero_index, zero_index),
    )
    head_dev = heads // groups
    summed, totals = (
        lax.psum_scatter(latent_sum, "sample", scatter_dimension=1, tiled=True),
        lax.psum_scatter(denom, "sample", scatter_dimension=1, tiled=True),
    )
    w_mine = lax.dynamic_slice_in_dim(w_uv, lax.axis_index("sample") * head_dev, head_dev, 0)
    mapped = jnp.einsum(
        "ghc,hcv->ghv", summed, w_mine.astype(jnp.float32), precision=lax.Precision.HIGHEST
    )
    values = mapped / totals[..., None]
    flat_values = values.reshape(group_tok, head_dev * vdim).astype(jnp.bfloat16)
    rows = flat_values
    attn = lax.psum_scatter(
        jnp.dot(rows, w_out, preferred_element_type=jnp.float32),
        "sample",
        scatter_dimension=0,
        tiled=True,
    )
    hidden = (residual.astype(jnp.float32) + attn).astype(jnp.bfloat16)
    hf = hidden.astype(jnp.float32)
    normed = (
        hf
        * lax.rsqrt(jnp.mean(hf * hf, axis=-1, keepdims=True) + norm_eps)
        * norm_gain.astype(jnp.float32)
    ).astype(jnp.bfloat16)
    logits = jnp.dot(normed, router, preferred_element_type=jnp.float32)
    experts = router.shape[1]
    top = expert_ids.shape[1]
    chosen_mask = jnp.any(
        expert_ids[:, :, None] == lax.iota(jnp.int32, experts)[None, None, :], axis=1
    ).astype(jnp.float32)
    chosen = jax.nn.sigmoid(logits) * chosen_mask
    gate = chosen / jnp.sum(chosen, axis=-1, keepdims=True) * route_scale
    earlier = (
        lax.iota(jnp.int32, tok_dev)[:, None] > lax.iota(jnp.int32, tok_dev)[None, :]
    ).astype(jnp.float32)
    rank = jnp.dot(earlier, chosen_mask, precision=lax.Precision.HIGHEST)
    capacity = (tok_dev * top + experts - 1) // experts + 1
    devices = lax.axis_size("prompt") * groups
    split = devices // experts
    slot_ids = lax.iota(jnp.int32, capacity).astype(jnp.float32)
    placed = chosen_mask.T[:, None, :] * (rank.T[:, None, :] == slot_ids[None, :, None]).astype(
        jnp.float32
    )
    outgoing = jnp.einsum(
        "ect,td->ecd", placed.astype(jnp.bfloat16), normed, preferred_element_type=jnp.float32
    ).astype(jnp.bfloat16)
    outgoing = jnp.broadcast_to(
        outgoing[:, None], (experts, split, capacity, normed.shape[1])
    ).reshape(devices, capacity, normed.shape[1])
    block = lax.all_to_all(outgoing, ("prompt", "sample"), split_axis=0, concat_axis=0, tiled=True)
    gate_part = jnp.einsum("fnd,du->fnu", block, w_gate[0], preferred_element_type=jnp.float32)
    up_part = jnp.einsum("fnd,du->fnu", block, w_up[0], preferred_element_type=jnp.float32)
    act = (jax.nn.silu(gate_part) * up_part).astype(jnp.bfloat16)
    part = jnp.einsum("fnu,ud->fnd", act, w_down[0], preferred_element_type=jnp.float32).astype(
        jnp.bfloat16
    )
    returned = lax.all_to_all(part, ("prompt", "sample"), split_axis=0, concat_axis=0, tiled=True)
    per_expert = jnp.sum(
        returned.reshape(experts, split, capacity, normed.shape[1]).astype(jnp.float32), axis=1
    )
    weighted = placed * gate.T[:, None, :]
    moe = jnp.einsum("ect,ecd->td", weighted, per_expert, precision=lax.Precision.HIGHEST)
    final = (hf + moe).astype(jnp.bfloat16)
    step_id = lax.iota(jnp.int32, tok_dev) % 2
    keep = jnp.where(step_id == 0, 1, jnp.repeat(accept[0], 2)).astype(jnp.bfloat16)
    rows = final * keep[:, None]
    targets = lax.dynamic_slice_in_dim(assign[0], start_row, tok_dev, 0)
    route_table = (lax.iota(jnp.int32, group_tok)[:, None] == targets[None, :]).astype(jnp.bfloat16)
    sending = jnp.dot(route_table, rows, preferred_element_type=jnp.float32).astype(jnp.bfloat16)
    sending = sending.reshape(groups, tok_dev, rows.shape[1])
    arrived = lax.all_to_all(sending, "sample", split_axis=0, concat_axis=0, tiled=True)
    return jnp.sum(arrived.astype(jnp.float32), axis=0).astype(jnp.bfloat16)


def solution(mesh):
    placed = (
        P(("prompt", "sample"), None, None),
        P(("prompt", "sample"), None),
        P("prompt", "sample", None),
        P(("prompt", "sample"), None),
        P(),
        P("sample", None),
        P(),
        P(),
        P(("prompt", "sample"), None),
        P(("prompt", "sample"), None, None),
        P(("prompt", "sample"), None, None),
        P(("prompt", "sample"), None, None),
        P("prompt", "sample"),
        P("prompt", None),
    )
    return jax.shard_map(
        local, mesh=mesh, in_specs=placed, out_specs=P(("prompt", "sample"), None), check_vma=False
    )
```

profile of v0, /device:TPU:0, one launch (start us, length us, event | category | flops | bytes accessed | tf_op | source)
XLA Modules:
  0.0 453.6 jit_solution(10266899996213429123)
XLA Ops:
  6.5 0.7 all-gather.2.cloned.1.call-update
  7.3 0.0 reduce-scatter.2.cloned.1.call-start
  7.3 3.1 copy.32
  10.4 0.2 select_reduce_fusion
  10.7 33.8 %all-gather.2.cloned.1.call-done = bf16[32,32,576]{2,1,0:T(8,128)(2,1)} async-done(((bf16[2,32,576]{2,1,0:T(8,128)(2,1)}), bf16[32,32,576]{2,1,0:T(8,128)(2,1)}) %all-gather.2.cloned.1.call-update) | async-done | bytes 1179664 | tf_op jit(solution)/shard_map/all_gather | solution.py:34
  44.5 8.7 %multiply_reduce_fusion = (f32[32,32]{1,0:T(8,128)S(1)}, f32[32,32,2048]{2,1,0:T(8,128)}) fusion(bf16[32,32,576]{2,1,0:T(8,128)(2,1)} %all-gather.2.cloned.1.call-done, bf16[1,2048,576]{1,2,0:T(8,128)(2,1)} %param.16), kind=kOutput, calls=%fused_computation.4 | convolution fusion | flops 2420112384 | bytes 11931648 | tf_op jit(solution)/shard_map/ghk,lk->ghl/dot_general | solution.py:37
  53.2 54.6 %pmax.7 = f32[32,32]{1,0:T(8,128)S(1)} all-reduce(f32[32,32]{1,0:T(8,128)S(1)} %max.5), channel_id=1, replica_groups=mesh['prompt'=8,'sample'=16] {'sample'}, use_global_device_ids=true, to_apply=%region_2.3 | all-reduce | flops 1024 | bytes 8192 | tf_op jit(solution)/shard_map/pmax | solution.py:53
  107.9 5.8 %fusion.5 = f32[32,32,512]{2,1,0:T(8,128)S(1)} fusion(f32[32,32,2048]{2,1,0:T(8,128)} %get-tuple-element.8, f32[32,32]{1,0:T(8,128)S(1)} %pmax.7, bf16[2048,576]{1,0:T(8,128)(2,1)S(1)} %bitcast.83), kind=kOutput, calls=%fused_computation.12 | convolution fusion | flops 2153775104 | bytes 12599296 | tf_op jit(solution)/shard_map/ghl,lc->ghc/dot_general | solution.py:63
  113.6 0.3 fusion.28
  113.9 2.6 copy.34
  116.5 0.0 reduce-scatter.2.cloned.1.call-update
  116.6 0.0 all-reduce.4.cloned.1.call-start
  116.6 0.6 dynamic-slice.3
  117.9 0.1 fusion.74
  118.0 4.3 fusion.3
  122.2 0.0 copy-start.8
  122.3 0.0 copy-start.3
  122.3 0.1 copy.35
  122.4 53.3 %all-reduce = f32[32,32]{0,1:T(8,128)S(1)} all-reduce(f32[32,32]{0,1:T(8,128)S(1)} %copy.35), channel_id=3, replica_groups=mesh['prompt'=8,'sample'=16] {'sample'}, use_global_device_ids=true, to_apply=%region_6.7.clone | all-reduce | flops 1024 | bytes 8192
  175.7 3.6 reduce-scatter.2.cloned.1.call-done
  179.2 1.2 fusion.31
  180.4 3.8 fusion.43
  184.2 0.0 all-reduce.4.cloned.1.call-update
  184.2 0.1 fusion.47
  184.3 0.1 fusion.53
  184.5 117.8 %all-reduce.4.cloned.1.call-done = f32[32,7168]{1,0:T(8,128)} async-done(((f32[32,7168]{1,0:T(8,128)}), f32[32,7168]{1,0:T(8,128)}) %all-reduce.4.cloned.1.call-update) | async-done | bytes 917520
  302.3 1.1 fusion.38
  303.4 0.4 convolution_convert_fusion.2
  303.8 0.5 copy.37
  304.3 1.9 broadcast_in_dim.29
  306.2 56.2 %all_to_all.15 = bf16[128,2,7168]{2,1,0:T(2,128)(2,1)S(1)} all-to-all(bf16[128,2,7168]{2,1,0:T(2,128)(2,1)S(1)} %bitcast.82), channel_id=1, replica_groups=mesh['prompt'=8,'sample'=16] {'prompt','sample'}, dimensions={0} | all-to-all | bytes 7340032 | tf_op jit(solution)/shard_map/all_to_all | solution.py:130
  362.4 1.1 fusion.12
  363.5 0.9 copy-done.7
  364.4 1.1 fusion.23
  365.6 0.9 copy-done.1
  366.5 1.1 convolution_convert_fusion
  367.6 5.6 %copy.40 = bf16[128,2,7168]{2,1,0:T(2,128)(2,1)} copy(bf16[128,2,7168]{2,0,1:T(8,128)(2,1)S(1)} %convolution_convert_fusion) | data formatting | bytes 7340032 | tf_op jit(solution)/shard_map/convert_element_type | solution.py:134
  373.2 6.1 %all-to-all-start.1 = ((bf16[128,2,7168]{2,1,0:T(2,128)(2,1)}), bf16[128,2,7168]{2,1,0:T(2,128)(2,1)}, u32[]{:S(2)}, u32[]{:S(2)}) async-start(bf16[128,2,7168]{2,1,0:T(2,128)(2,1)} %copy.40), calls=%async_computation.2 | async-start | bytes 7340032 | tf_op jit(solution)/shard_map/all_to_all | solution.py:137
  380.0 0.1 fusion.70
  380.1 0.4 fusion.78
  380.5 0.1 multiply_bitcast_fusion
  380.5 45.3 %all-to-all-done.1 = bf16[128,2,7168]{2,1,0:T(2,128)(2,1)} async-done(((bf16[128,2,7168]{2,1,0:T(2,128)(2,1)}), bf16[128,2,7168]{2,1,0:T(2,128)(2,1)}, u32[]{:S(2)}, u32[]{:S(2)}) %all-to-all-start.1) | async-done | bytes 3670048 | tf_op jit(solution)/shard_map/all_to_all | solution.py:137
  425.8 5.7 %convert_reduce_fusion = f32[16,2,7168]{2,1,0:T(2,128)S(1)} fusion(bf16[128,2,7168]{2,1,0:T(2,128)(2,1)} %all-to-all-done.1), kind=kLoop, calls=%fused_computation.9 | loop fusion | flops 3440640 | bytes 4587520 | tf_op jit(solution)/shard_map/reduce_sum | solution.py:138
  431.6 0.9 fusion.2
  432.5 0.3 convolution_convert_fusion.1
  432.7 0.2 reshape.101
  432.9 13.1 %all_to_all.16 = bf16[16,2,7168]{2,1,0:T(2,128)(2,1)S(1)} all-to-all(bf16[16,2,7168]{2,1,0:T(2,128)(2,1)S(1)} %reshape.101), channel_id=1, replica_groups=mesh['prompt'=8,'sample'=16] {'sample'}, dimensions={0} | all-to-all | bytes 917504 | tf_op jit(solution)/shard_map/all_to_all | solution.py:151
  446.0 1.0 reduce_sum.65
  (31 shorter events, 0.1 us)
Async XLA Ops:
  6.5 373.5 %copy-start = (bf16[7168,16]{0,1:T(8,128)(2,1)S(1)}, bf16[7168,16]{0,1:T(8,128)(2,1)}, u32[]{:S(2)}) copy-start(bf16[7168,16]{0,1:T(8,128)(2,1)} %param.21) | copy-start | bytes 688132
  6.5 3.9 copy-start.2
  6.5 3.9 copy-start.5
  6.5 38.0 %all-gather.2.cloned.1.call-start = ((), (), s32[]{:S(2)}) async-start(), calls=%async_computation.4 | async-start | bytes 1392640 | tf_op jit(solution)/shard_map/all_gather | solution.py:34
  7.3 171.9 %reduce-scatter.2.cloned.1.call-start = ((), (), s32[]{:S(2)}) async-start(), calls=%async_computation.5 | async-start | bytes 2228224 | tf_op jit(solution)/shard_map/reduce_scatter | solution.py:82
  113.6 3.0 copy-start.10
  116.6 185.7 %all-reduce.4.cloned.1.call-start = ((), (), s32[]{:S(2)}) async-start(), calls=%async_computation.6 | async-start | bytes 1835008
  122.2 62.0 %copy-start.4 = (bf16[7168]{0:T(1024)(128)(2,1)S(1)}, bf16[7168]{0:T(1024)(128)(2,1)}, u32[]{:S(2)}) copy-start(bf16[7168]{0:T(1024)(128)(2,1)} %param.20) | copy-start | bytes 43012
  122.2 62.0 %copy-start.8 = (s32[2,8]{1,0:T(2,128)S(1)}, s32[2,8]{1,0:T(2,128)}, u32[]{:S(2)}) copy-start(s32[2,8]{1,0:T(2,128)} %param.22) | copy-start | bytes 196
  122.3 180.0 %copy-start.3 = (bf16[2,7168]{1,0:T(2,128)(2,1)S(1)}, bf16[2,7168]{1,0:T(2,128)(2,1)}, u32[]{:S(2)}) copy-start(bf16[2,7168]{1,0:T(2,128)(2,1)} %param.17) | copy-start | bytes 86020
  306.2 56.2 %copy-start.6 = (bf16[1,7168,256]{2,1,0:T(8,128)(2,1)S(1)}, bf16[1,7168,256]{2,1,0:T(8,128)(2,1)}, u32[]{:S(2)}) copy-start(bf16[1,7168,256]{2,1,0:T(8,128)(2,1)} %param.23) | copy-start | bytes 11010052
  362.4 2.0 copy-start.7
  364.4 2.0 copy-start.1
  373.2 6.8 %copy-start.9 = (s32[1,32]{1,0:T(1,128)S(1)}, s32[1,32]{1,0:T(1,128)}, u32[]{:S(2)}) copy-start(s32[1,32]{1,0:T(1,128)} %param.27) | copy-start | bytes 388
  373.2 52.6 %all-to-all-start.1 = ((bf16[128,2,7168]{2,1,0:T(2,128)(2,1)}), bf16[128,2,7168]{2,1,0:T(2,128)(2,1)}, u32[]{:S(2)}, u32[]{:S(2)}) async-start(bf16[128,2,7168]{2,1,0:T(2,128)(2,1)} %copy.40), calls=%async_computation.2 | async-start | bytes 7340032 | tf_op jit(solution)/shard_map/all_to_all | solution.py:137
Sparse Core Ops, SparseCore 0:
  9.1 35.3 all-gather.1
  116.7 62.4 reduce-scatter.1
  184.3 117.8 all-reduce.3
where the time goes:
time: 454 us
  waiting for transfers between devices  201 us (44%)
  blocking collectives  177 us (39%)
  matrix products  25.3 us (6%)
  local copies, waits for them, and re-layouts  16.5 us (4%)
  between operations  14.7 us (3%)
  other arithmetic  12.4 us (3%)
  starting transfers between devices  6.18 us (1%)
    unnamed x4, waiting for transfers between devices  119 us
    all_to_all x1, blocking collectives, local(): lax.all_to_all(outgoing, ('prompt', 'sample'), split_axis=0, concat_axis=...  56.2 us
    pmax x1, blocking collectives, local(): shift = lax.pmax(local_peak, 'sample')  54.6 us
    unnamed x1, blocking collectives  53.3 us
    all_to_all x1, waiting for transfers between devices, local(): lax.all_to_all(part, ('prompt', 'sample'), split_axis=0, concat_axis=0, t...  45.3 us
    all_gather x1, waiting for transfers between devices, local(): every_query = lax.all_gather(queries, 'sample', axis=0, tiled=True)  33.8 us
    all_to_all x1, blocking collectives, local(): lax.all_to_all(sending, 'sample', split_axis=0, concat_axis=0, tiled=True)  13.1 us
  transfers between devices with their start and end apart: 4, of which 4 were waited for; matrix products, arithmetic and copies ran while one was open for 2% of the time, Pallas kernels for 0%

commit v1 on v0

v1 whole, which is shorter than its diff:
```python
import functools
import jax
import jax.numpy as jnp
from jax import lax
from jax.experimental import pallas as pl
from jax.experimental.pallas import tpu as pltpu
from jax.sharding import PartitionSpec as P

MESH = pl.DeviceIdType.MESH
F32 = jnp.float32
BF16 = jnp.bfloat16
score_scale = 192.0 ** (-0.5)
log2e = 1.4426950408889634
route_scale = 2.827
norm_eps = 1e-06

COLS = 896
PIECES = ((384, 384, "xzy"), (384, 256, "yxz"), (256, 256, "zyx"))


def nt(a, b):
    return lax.dot_general(a, b, (((1,), (1,)), ((), ())), preferred_element_type=F32)


def mm(a, b):
    return jnp.dot(a, b, preferred_element_type=F32)


class Links:
    def __init__(self, send_sem, recv_sem, anyone):
        self.send_sem, self.recv_sem, self.anyone = send_sem, recv_sem, anyone
        self.sent, self.taken = [], 0

    def slots(self, n=1):
        self.taken += n
        return self.taken - n

    def send(self, src, dst, slot, device):
        copy = pltpu.make_async_remote_copy(
            src_ref=src,
            dst_ref=dst,
            send_sem=self.send_sem.at[len(self.sent)],
            recv_sem=self.recv_sem.at[slot],
            device_id=device,
            device_id_type=MESH,
        )
        copy.start()
        self.sent.append(copy)

    def arrived(self, dst, slot):
        pltpu.make_async_remote_copy(
            src_ref=dst,
            dst_ref=dst,
            send_sem=self.send_sem.at[0],
            recv_sem=self.recv_sem.at[slot],
            device_id=self.anyone,
            device_id_type=MESH,
        ).wait_recv()

    def finish(self):
        for copy in self.sent:
            copy.wait_send()


def kernel(
    q_in,
    cache_in,
    uv_in,
    out_in,
    router_in,
    gate_in,
    up_in,
    down_in,
    new_keys,
    residual,
    gain,
    ids,
    accept,
    assign,
    result,
    kc,
    wuv,
    wout,
    wgate,
    wup,
    wdown,
    rpad,
    qbuf,
    kn,
    obuf,
    vsend,
    vrecv,
    asend,
    arecv,
    hbuf,
    xa,
    xb,
    xc,
    pa,
    pb,
    pc,
    r0a,
    r0b,
    r0c,
    r1a,
    r1b,
    r1c,
    r2a,
    r2b,
    r2c,
    r3a,
    r3b,
    r3c,
    f1,
    f2,
    fsend,
    frecv,
    load_sem,
    send_sem,
    recv_sem,
):
    p = lax.axis_index("prompt")
    s = lax.axis_index("sample")
    x, zh = p // 2, p % 2
    y, zl, k = s // 4, (s // 2) % 2, s % 2
    z = zh * 2 + zl
    chip = y * 2 + zl
    at = {"x": x, "y": y, "z": z}

    def device(x, y, z, k):
        return (x * 2 + z // 2, y * 4 + (z % 2) * 2 + k)

    def peer(axis, step):
        there = dict(at)
        there[axis] = (at[axis] + step) % 4
        return device(there["x"], there["y"], there["z"], k)

    def member(t):
        return (p, t)

    other = (p, y * 4 + zl * 2 + (1 - k))
    across = (p, y * 4 + (1 - zl) * 2 + k)

    loads = []
    first_column = pl.multiple_of(chip * COLS, 128)
    for n, (src, dst) in enumerate(
        (
            (q_in, qbuf.at[s]),
            (cache_in, kc),
            (uv_in, wuv),
            (out_in, wout),
            (router_in.at[:, pl.ds(first_column, COLS)], rpad.at[pl.ds(0, 16)]),
            (gate_in, wgate),
            (up_in, wup),
            (down_in, wdown),
        )
    ):
        loads.append(pltpu.make_async_copy(src, dst, load_sem.at[n]))
        loads[-1].start()

    barrier = pltpu.get_barrier_semaphore()
    partners = [member((s + r) % 16) for r in range(1, 16)]
    partners += [peer("x", r) for r in (1, 2, 3)]
    partners += [device(x, y, (1 - zh) * 2 + r, k) for r in (0, 1)]
    for there in partners:
        pl.semaphore_signal(barrier, inc=1, device_id=there, device_id_type=MESH)
    pl.semaphore_wait(barrier, len(partners))

    links = Links(send_sem, recv_sem, other)
    send, arrived, slots = links.send, links.arrived, links.slots

    q_slot = slots(16)
    y_left, y_right, y_far = (y + 3) % 4, (y + 1) % 4, (y + 2) % 4

    def q_send(t, there):
        send(qbuf.at[t], qbuf.at[t], q_slot + t, there)

    def q_arrived(t):
        arrived(qbuf.at[t], q_slot + t)

    def q_at(yy, zz, kk):
        return yy * 4 + zz * 2 + kk

    here, beside = q_at(y, zl, k), q_at(y, 1 - zl, k)
    loads[0].wait()
    q_send(here, across)
    q_send(here, peer("y", 1))
    q_send(here, peer("y", 3))
    q_send(here, other)

    rows16 = lax.broadcasted_iota(jnp.int32, (128, 576), 0)
    fresh = new_keys[...].astype(F32)
    kn[...] = jnp.where(
        rows16 == 0, fresh[0:1, :], jnp.where(rows16 == 1, fresh[1:2, :], 0.0)
    ).astype(BF16)
    rpad[pl.ds(16, 112)] = jnp.zeros((112, COLS), BF16)

    q_arrived(beside)
    q_send(beside, peer("y", 1))
    q_send(beside, peer("y", 3))
    q_send(beside, other)
    left_own, left_beside = q_at(y_left, zl, k), q_at(y_left, 1 - zl, k)
    right_own, right_beside = q_at(y_right, zl, k), q_at(y_right, 1 - zl, k)
    far_own, far_beside = q_at(y_far, zl, k), q_at(y_far, 1 - zl, k)
    q_arrived(left_own)
    q_send(left_own, peer("y", 1))
    q_send(left_own, other)
    q_arrived(right_own)
    q_send(right_own, other)
    q_arrived(q_at(y, zl, 1 - k))
    q_arrived(q_at(y, 1 - zl, 1 - k))

    to_log2 = score_scale * log2e

    def attend(yy, own):
        q = qbuf[pl.ds(yy * 4, 4)].reshape(256, 576)
        scores = mm(q, kc[...]) * to_log2
        peak = jnp.max(scores, axis=1, keepdims=True)
        if own:
            row = lax.broadcasted_iota(jnp.int32, (256, 128), 0) - (zl * 2 + k) * 64
            column = lax.broadcasted_iota(jnp.int32, (256, 128), 1)
            seen = ((row >= 0) & (row < 64) & (column == 0)) | (
                (row >= 32) & (row < 64) & (column == 1)
            )
            own_scores = jnp.where(seen, nt(q, kn[...]) * to_log2, -jnp.inf)
            peak = jnp.maximum(peak, jnp.max(own_scores, axis=1, keepdims=True))
        weights = jnp.exp2(scores - peak)
        denom = jnp.sum(weights, axis=1, keepdims=True)
        latent = nt(weights.astype(BF16), kc[pl.ds(0, 512), :])
        if own:
            own_weights = jnp.exp2(own_scores - peak)
            denom = denom + jnp.sum(own_weights, axis=1, keepdims=True)
            latent = latent + mm(own_weights.astype(BF16), kn[:, pl.ds(0, 512)])
        at_rows = pl.ds(pl.multiple_of(yy * 256, 256), 256)
        latent = latent / denom
        for n in range(4):
            obuf[n, at_rows, :] = latent[:, n * 128 : (n + 1) * 128]
        obuf[4, at_rows, :] = jnp.broadcast_to(peak + jnp.log2(denom), (256, 128))

    loads[1].wait()
    attend(y, True)
    q_arrived(left_beside)
    q_send(left_beside, other)
    q_arrived(right_beside)
    q_send(right_beside, peer("y", 3))
    q_send(right_beside, other)
    q_arrived(q_at(y_left, zl, 1 - k))
    q_arrived(q_at(y_left, 1 - zl, 1 - k))
    attend(y_left, False)
    q_arrived(far_own)
    q_send(far_own, other)
    q_arrived(far_beside)
    q_send(far_beside, other)
    q_arrived(q_at(y_right, zl, 1 - k))
    q_arrived(q_at(y_right, 1 - zl, 1 - k))
    attend(y_right, False)
    q_arrived(q_at(y_far, zl, 1 - k))
    q_arrived(q_at(y_far, 1 - zl, 1 - k))
    attend(y_far, False)

    lane32 = lax.broadcasted_iota(jnp.int32, (32, 128), 1)
    row32 = lax.broadcasted_iota(jnp.int32, (32, 128), 0)
    facts = jnp.zeros((32, 128), F32)
    own_ids = ids[...]
    targets = assign[...]
    spots = lax.broadcasted_iota(jnp.int32, (1, 32), 1)
    for t in range(2):
        mark = jnp.zeros((32, 128), F32)
        for j in range(8):
            mark = mark + jnp.where(lane32 == own_ids[t : t + 1, j : j + 1] + 16, 0.125, 0.0)
        target = jnp.sum(
            jnp.where(spots == 2 * s + t, targets.astype(F32), 0.0), axis=1, keepdims=True
        )
        mark = mark + jnp.where(lane32 == 32, target * 0.125, 0.0)
        keep = jnp.ones((1, 1), F32) if t == 0 else accept[...].astype(F32)
        mark = mark + jnp.where(lane32 == 33, keep * 0.125, 0.0)
        facts = jnp.where(row32 == t, mark, facts)

    v_slot = slots(16)
    loads[2].wait()
    for r in (8, 10, 9, 11, 4, 12, 5, 13, 6, 14, 7, 15, 2, 3, 1, 0):
        owner = (s + r) % 16
        stats = facts
        halves = []
        for j in range(2):
            head = owner * 2 + j
            mine = [obuf[n, pl.ds(head, 32, stride=32), :] for n in range(5)]
            latent = jnp.concatenate(mine[:4], axis=1).astype(BF16)
            halves.append(mm(latent, wuv[head]).astype(BF16))
            level = mine[4]
            high = level.astype(BF16).astype(F32)
            middle = (level - high).astype(BF16).astype(F32)
            low = level - high - middle
            stats = jnp.where(lane32 == j * 64, high, stats)
            stats = jnp.where(lane32 == j * 64 + 1, middle, stats)
            stats = jnp.where(lane32 == j * 64 + 2, low, stats)
        message = jnp.concatenate(halves + [stats.astype(BF16)], axis=1)
        if r == 0:
            vrecv[s] = message
        else:
            vsend[r] = message
            send(vsend.at[r], vrecv.at[s], v_slot + s, member(owner))
    for r in range(1, 16):
        source = (s + r) % 16
        arrived(vrecv.at[source], v_slot + source)

    lane3 = lax.broadcasted_iota(jnp.int32, (16, 32, 128), 2)
    got = vrecv[:, :, pl.ds(256, 128)].astype(F32)
    values = []
    for j in range(2):
        inside = (lane3 >= j * 64) & (lane3 < j * 64 + 3)
        level = jnp.sum(jnp.where(inside, got, 0.0), axis=2, keepdims=True)
        share = jnp.exp2(level - jnp.max(level, axis=0, keepdims=True))
        total = jnp.sum(share, axis=0)
        heard = vrecv[:, :, pl.ds(j * 128, 128)].astype(F32)
        values.append(jnp.sum(heard * share, axis=0) / total)
    values = jnp.concatenate(values, axis=1).astype(BF16)

    pick_row = lax.broadcasted_iota(jnp.int32, (16, 128), 0)
    pick_lane = lax.broadcasted_iota(jnp.int32, (16, 128), 1)
    pick = (pick_lane == (pick_row >> 1) * 16 + (pick_row & 1)).astype(BF16)
    told = vrecv[pl.ds(k * 8, 8), pl.ds(0, 16), pl.ds(256, 128)].reshape(128, 128)
    facts = mm(pick, told)
    facts = jnp.where((pick_lane >= 16) & (pick_lane < 34), facts, 0.0)
    keep = jnp.sum(jnp.where(pick_lane == 33, facts, 0.0), axis=1, keepdims=True) * 8.0

    a_slot = slots(16)
    loads[3].wait()
    row_wide = lax.broadcasted_iota(jnp.int32, (32, COLS), 0)
    for dy in (2, 1, 3, 0):
        for dz in (1, 0):
            c = ((y + dy) % 4) * 2 + (zl + dz) % 2
            columns = pl.ds(pl.multiple_of(c * COLS, 128), COLS)
            part = mm(values, wout[:, columns])
            rest = residual[:, columns].astype(F32)
            part = part + jnp.where(
                row_wide == 2 * s,
                rest[0:1, :],
                jnp.where(row_wide == 2 * s + 1, rest[1:2, :], 0.0),
            )
            part = part.astype(BF16)
            n = (dy * 2 + dz) * 2
            asend[n] = part[:16]
            asend[n + 1] = part[16:]
            far = (dy, dz) != (0, 0)
            if far:
                for kk in range(2):
                    send(asend.at[n + kk], arecv.at[s], a_slot + s, member(c * 2 + kk))
            else:
                send(asend.at[n + 1 - k], arecv.at[s], a_slot + s, other)
                arecv[s] = asend[n + k]
    for r in range(1, 16):
        source = (s + r) % 16
        arrived(arecv.at[source], a_slot + source)
    hidden = jnp.sum(arecv[...].astype(F32), axis=0).astype(BF16).astype(F32)

    h_slot = slots(1)
    hbuf[k] = (hidden * keep).astype(BF16)
    send(hbuf.at[k], hbuf.at[k], h_slot, other)

    loads[4].wait()
    block = (hidden * gain[:, pl.ds(first_column, COLS)].astype(F32)).astype(BF16)
    squares = jnp.sum(hidden * hidden, axis=1, keepdims=True)
    squares_high = squares.astype(BF16).astype(F32)
    logits = nt(block, rpad[...])
    logits_high = logits.astype(BF16).astype(F32)
    note = logits_high + pltpu.roll(logits - logits_high, 16, 1) + pltpu.roll(facts, 32, 1)
    note = note + jnp.where(pick_lane == 32, squares_high, 0.0)
    note = note + jnp.where(pick_lane == 33, squares - squares_high, 0.0)
    tail = jnp.concatenate([block[:, 768:], note.astype(BF16)], axis=1)
    gathered = (xa, xb, xc)
    for buf, (w, _, order), piece in zip(
        gathered, PIECES, (block[:, :384], block[:, 384:768], tail)
    ):
        c1, c2, c3 = (at[axis] for axis in order)
        buf[k, c3, c2, c1] = piece

    plan = []
    for buf, (w, _, order) in zip(gathered, PIECES):
        plan.append((buf, order, tuple(at[axis] for axis in order), slots(3), slots(3), slots(6), slots(7)))
    for buf, order, (c1, c2, c3), s1, s2, s3, s4 in plan:
        mine = buf.at[k, c3, c2, c1]
        for o in (2, 1, 3):
            send(mine, mine, s1 + o - 1, peer(order[0], o))
    for buf, order, (c1, c2, c3), s1, s2, s3, s4 in plan:
        for o in (1, 3, 2):
            arrived(buf.at[k, c3, c2, (c1 + 4 - o) % 4], s1 + o - 1)
        mine = buf.at[k, c3, c2]
        for o in (2, 1, 3):
            send(mine, mine, s2 + o - 1, peer(order[1], o))

    def half(buf, plane, c3, h):
        return buf.at[plane, c3, pl.ds(2 * h, 2)]

    for buf, order, (c1, c2, c3), s1, s2, s3, s4 in plan:
        for o in (1, 3, 2):
            arrived(buf.at[k, c3, (c2 + 4 - o) % 4], s2 + o - 1)
        for h, o in ((0, 1), (1, 3), (1, 1), (0, 3)):
            mine = half(buf, k, c3, h)
            send(mine, mine, s3 + (0 if o == 1 else 2) + h, peer(order[2], o))
        send(buf.at[k, c3], buf.at[k, c3], s4 + 6, other)
    for step in range(3):
        for buf, order, (c1, c2, c3), s1, s2, s3, s4 in plan:
            left, right, far = (c3 + 3) % 4, (c3 + 1) % 4, (c3 + 2) % 4
            for n, c, h, onward in (
                ((0, left, 0, 1), (3, right, 1, 3)),
                ((1, left, 1, 0), (2, right, 0, 0)),
                ((4, far, 0, 0), (5, far, 1, 0)),
            )[step]:
                view = half(buf, k, c, h)
                arrived(view, s3 + n)
                if onward:
                    send(view, view, s3 + 4 + h, peer(order[2], onward))
                send(view, view, s4 + n, other)
    for buf, order, (c1, c2, c3), s1, s2, s3, s4 in plan:
        left, right, far = (c3 + 3) % 4, (c3 + 1) % 4, (c3 + 2) % 4
        arrived(buf.at[1 - k, c3], s4 + 6)
        for n, c, h in (
            (0, left, 0), (3, right, 1), (1, left, 1), (2, right, 0), (4, far, 0), (5, far, 1)
        ):
            arrived(half(buf, 1 - k, c, h), s4 + n)

    def rows_of(buf, order, yy, zz, columns):
        blocks = []
        for kk in range(2):
            for hh in range(2):
                for xx in range(4):
                    c = {"x": xx, "y": yy, "z": hh * 2 + zz}
                    c1, c2, c3 = (c[axis] for axis in order)
                    blocks.append(buf[kk, c3, c2, c1, :, columns])
        return jnp.concatenate(blocks, axis=0)

    note = jnp.zeros((256, 128), F32)
    gate_part = jnp.zeros((256, 256), F32)
    up_part = jnp.zeros((256, 256), F32)
    loads[5].wait()
    loads[6].wait()
    for yy in range(4):
        for zz in range(2):
            c = yy * 2 + zz
            tokens = jnp.concatenate(
                [
                    rows_of(xa, "xzy", yy, zz, pl.ds(0, 384)),
                    rows_of(xb, "yxz", yy, zz, pl.ds(0, 384)),
                    rows_of(xc, "zyx", yy, zz, pl.ds(0, 128)),
                ],
                axis=1,
            )
            note = note + rows_of(xc, "zyx", yy, zz, pl.ds(128, 128)).astype(F32)
            gate_part = gate_part + mm(tokens, wgate[pl.ds(c * COLS, COLS), :])
            up_part = up_part + mm(tokens, wup[pl.ds(c * COLS, COLS), :])

    lane = lax.broadcasted_iota(jnp.int32, (256, 128), 1)
    row = lax.broadcasted_iota(jnp.int32, (256, 128), 0)

    def column_sum(inside):
        return jnp.sum(jnp.where(inside, note, 0.0), axis=1, keepdims=True)

    model_width = 8 * COLS
    scale = lax.rsqrt(column_sum((lane == 32) | (lane == 33)) / model_width + norm_eps)
    logits = (note + pltpu.roll(note, 112, 1)) * scale
    chosen = jnp.where(lane < 16, jax.nn.sigmoid(logits) * pltpu.roll(note, 80, 1), 0.0)
    expert = (p * 16 + s) // 8
    gate = jnp.sum(jnp.where(lane == expert, chosen, 0.0), axis=1, keepdims=True)
    gate = gate / jnp.sum(chosen, axis=1, keepdims=True) * route_scale
    gate = gate * column_sum(lane == 65)
    act = jax.nn.silu(gate_part * scale) * (up_part * scale) * gate
    target = jnp.broadcast_to(column_sum(lane == 64), (256, 128)).astype(jnp.int32)
    place = ((target >> 1) & 1) * 128 + (row & 112) + (target >> 2) * 2 + (target & 1)
    place = jnp.transpose(place.astype(F32))[0:1, :]
    move = (lax.broadcasted_iota(jnp.int32, (256, 256), 0).astype(F32) == place).astype(BF16)
    act = mm(move, act.astype(BF16)).astype(BF16)

    loads[7].wait()
    partial = (pa, pb, pc)
    for yy in range(4):
        for zz in range(2):
            c = yy * 2 + zz
            part = mm(act, wdown[:, pl.ds(c * COLS, COLS)]).astype(BF16)
            start = 0
            for buf, (_, w, order) in zip(partial, PIECES):
                for kk in range(2):
                    for hh in range(2):
                        for xx in range(4):
                            at_block = {"x": xx, "y": yy, "z": hh * 2 + zz}
                            c1, c2, c3 = (at_block[axis] for axis in order)
                            first = ((kk * 2 + hh) * 4 + xx) * 16
                            buf[kk, c3, c2, c1] = part[first : first + 16, start : start + w]
                start += w

    plan = []
    for n, (_, w, order) in enumerate(PIECES):
        bufs = (partial[n], (r0a, r0b, r0c)[n], (r1a, r1b, r1c)[n])
        bufs += ((r2a, r2b, r2c)[n], (r3a, r3b, r3c)[n])
        plan.append((bufs, order, tuple(at[axis] for axis in order), slots(1), slots(6), slots(3), slots(3)))

    def add_to(ref, *terms):
        total = ref[...].astype(F32)
        for term in terms:
            total = total + term[...].astype(F32)
        ref[...] = total.astype(BF16)

    for (part, r0, r1, r2, r3), order, cs, s0, s1, s2, s3 in plan:
        send(part.at[1 - k], r0, s0, other)
    for (part, r0, r1, r2, r3), order, (c1, c2, c3), s0, s1, s2, s3 in plan:
        left, right, far = (c3 + 3) % 4, (c3 + 1) % 4, (c3 + 2) % 4
        arrived(r0, s0)
        for c in (far, right, left, c3):
            add_to(part.at[k, c], r0.at[c])
        to_right, to_left = peer(order[2], 1), peer(order[2], 3)
        send(half(part, k, far, 0), r1.at[0], s1, to_right)
        send(half(part, k, far, 1), r1.at[1], s1 + 1, to_left)
        send(half(part, k, right, 1), r1.at[2], s1 + 2, to_right)
        send(half(part, k, left, 0), r1.at[3], s1 + 3, to_left)
    for (part, r0, r1, r2, r3), order, (c1, c2, c3), s0, s1, s2, s3 in plan:
        left, right = (c3 + 3) % 4, (c3 + 1) % 4
        arrived(r1.at[0], s1)
        add_to(half(part, k, right, 0), r1.at[0])
        send(half(part, k, right, 0), r1.at[4], s1 + 4, peer(order[2], 1))
        arrived(r1.at[1], s1 + 1)
        add_to(half(part, k, left, 1), r1.at[1])
        send(half(part, k, left, 1), r1.at[5], s1 + 5, peer(order[2], 3))
    for (part, r0, r1, r2, r3), order, (c1, c2, c3), s0, s1, s2, s3 in plan:
        for n in (2, 3, 4, 5):
            arrived(r1.at[n], s1 + n)
        add_to(half(part, k, c3, 0), r1.at[3], r1.at[4])
        add_to(half(part, k, c3, 1), r1.at[2], r1.at[5])
        for o in (2, 1, 3):
            send(part.at[k, c3, (c2 + o) % 4], r2.at[o - 1], s2 + o - 1, peer(order[1], o))
    for (part, r0, r1, r2, r3), order, (c1, c2, c3), s0, s1, s2, s3 in plan:
        for o in (1, 2, 3):
            arrived(r2.at[o - 1], s2 + o - 1)
        add_to(part.at[k, c3, c2], r2.at[0], r2.at[1], r2.at[2])
        for o in (2, 1, 3):
            send(part.at[k, c3, c2, (c1 + o) % 4], r3.at[o - 1], s3 + o - 1, peer(order[0], o))
    sums = []
    for (part, r0, r1, r2, r3), order, (c1, c2, c3), s0, s1, s2, s3 in plan:
        for o in (1, 2, 3):
            arrived(r3.at[o - 1], s3 + o - 1)
        sums.append(part[k, c3, c2, c1].astype(F32) + jnp.sum(r3[...].astype(F32), axis=0))

    arrived(hbuf.at[1 - k], h_slot)
    i = lax.broadcasted_iota(jnp.int32, (16, 32), 0)
    move = ((i >> 1) * 4 + k * 2 + (i & 1) == targets).astype(BF16)
    final = jnp.concatenate(sums, axis=1) + mm(move, hbuf[...].reshape(32, COLS))
    for j in range(7):
        f1[j] = final[:, j * 128 : (j + 1) * 128]

    f2[...] = jnp.zeros_like(f2)
    for t in range(2):
        for j in range(7):
            f2[pl.ds(t * 7 + j, 8, stride=16), :] = f1[j, pl.ds(t, 8, stride=2), :]
    fsend[...] = f2[...].reshape(8, 16, 128).astype(BF16)
    f_slot = slots(8)
    for r in range(1, 8):
        c = (chip + r) % 8
        send(fsend.at[c], frecv.at[chip], f_slot + chip, member(c * 2 + k))
    frecv[chip] = fsend[chip]
    for r in range(1, 8):
        c = (chip + r) % 8
        arrived(frecv.at[c], f_slot + c)
    result[...] = frecv[...]
    links.finish()


def local(
    queries,
    new_keys,
    cache,
    residual,
    w_uv,
    w_out,
    norm_gain,
    router,
    expert_ids,
    w_gate,
    w_up,
    w_down,
    accept,
    assign,
):
    positions = cache.shape[1]
    whole = pl.BlockSpec(memory_space=pltpu.VMEM)
    left = pl.BlockSpec(memory_space=pl.ANY)
    scratch = [
        pltpu.VMEM((576, positions), BF16),
        pltpu.VMEM((32, 512, 128), BF16),
        pltpu.VMEM((256, 7168), BF16),
        pltpu.VMEM((7168, 256), BF16),
        pltpu.VMEM((7168, 256), BF16),
        pltpu.VMEM((256, 7168), BF16),
        pltpu.VMEM((128, COLS), BF16),
        pltpu.VMEM((16, 64, 576), BF16),
        pltpu.VMEM((128, 576), BF16),
        pltpu.VMEM((5, 1024, 128), F32),
        pltpu.VMEM((16, 32, 384), BF16),
        pltpu.VMEM((16, 32, 384), BF16),
        pltpu.VMEM((16, 16, COLS), BF16),
        pltpu.VMEM((16, 16, COLS), BF16),
        pltpu.VMEM((2, 16, COLS), BF16),
    ]
    scratch += [pltpu.VMEM((2, 4, 4, 4, 16, w), BF16) for w, _, _ in PIECES]
    scratch += [pltpu.VMEM((2, 4, 4, 4, 16, w), BF16) for _, w, _ in PIECES]
    scratch += [pltpu.VMEM((4, 4, 4, 16, w), BF16) for _, w, _ in PIECES]
    scratch += [pltpu.VMEM((6, 2, 4, 16, w), BF16) for _, w, _ in PIECES]
    scratch += [pltpu.VMEM((3, 4, 16, w), BF16) for _, w, _ in PIECES]
    scratch += [pltpu.VMEM((3, 16, w), BF16) for _, w, _ in PIECES]
    scratch += [
        pltpu.VMEM((7, 16, 128), F32),
        pltpu.VMEM((128, 128), F32),
        pltpu.VMEM((8, 16, 128), BF16),
        pltpu.VMEM((8, 16, 128), BF16),
        pltpu.SemaphoreType.DMA((8,)),
        pltpu.SemaphoreType.DMA((192,)),
        pltpu.SemaphoreType.DMA((192,)),
    ]
    rows = pl.pallas_call(
        kernel,
        out_shape=jax.ShapeDtypeStruct((8, 16, 128), BF16),
        in_specs=[left] * 8 + [whole] * 6,
        out_specs=whole,
        scratch_shapes=scratch,
        compiler_params=pltpu.CompilerParams(
            collective_id=0, has_side_effects=True, vmem_limit_bytes=60 * 1024 * 1024
        ),
        name="layer",
    )(
        queries.reshape(64, 576),
        cache[0].T,
        w_uv,
        w_out,
        router.T,
        w_gate[0],
        w_up[0],
        w_down[0],
        new_keys,
        residual,
        norm_gain.reshape(1, 7168),
        expert_ids,
        accept,
        assign,
    )
    rows = rows[:, :14].reshape(8, 2, 7, 128).transpose(1, 0, 2, 3)
    return rows.reshape(2, 7168)


def solution(mesh):
    placed = (
        P(("prompt", "sample"), None, None),
        P(("prompt", "sample"), None),
        P("prompt", "sample", None),
        P(("prompt", "sample"), None),
        P(),
        P("sample", None),
        P(),
        P(),
        P(("prompt", "sample"), None),
        P(("prompt", "sample"), None, None),
        P(("prompt", "sample"), None, None),
        P(("prompt", "sample"), None, None),
        P("prompt", "sample"),
        P("prompt", None),
    )
    return jax.shard_map(
        local, mesh=mesh, in_specs=placed, out_specs=P(("prompt", "sample"), None), check_vma=False
    )
```

time: 454 us -> 93.9 us (0.21)
  waiting for transfers between devices: 201 us -> 0 us
  blocking collectives: 177 us -> 0 us
  Pallas kernels: 0 us -> 90.2 us
  matrix products: 25.3 us -> 0 us
  between operations: 14.7 us -> 0.66 us
  local copies, waits for them, and re-layouts: 16.5 us -> 2.75 us
  other arithmetic: 12.4 us -> 0 us
  starting transfers between devices: 6.18 us -> 0 us
    unnamed x4 -> x0, waiting for transfers between devices: 119 us -> none
    pallas_call x0 -> x1, Pallas kernels: none -> 90.2 us  [local(): pl.pallas_call(kernel, out_shape=jax.ShapeDtypeStruct((8, 16, 128), BF16)...]
    all_to_all x2 -> x0, blocking collectives: 69.3 us -> none  [the longest x1 56.2 us: local(): lax.all_to_all(outgoing, ('prompt', 'sample'), split_axis=0, concat_axis=...]
    pmax x1 -> x0, blocking collectives: 54.6 us -> none  [local(): shift = lax.pmax(local_peak, 'sample')]
    unnamed x1 -> x0, blocking collectives: 53.3 us -> none
    all_to_all x1 -> x0, waiting for transfers between devices: 45.3 us -> none  [local(): lax.all_to_all(part, ('prompt', 'sample'), split_axis=0, concat_axis=0, t...]
    all_gather x1 -> x0, waiting for transfers between devices: 33.8 us -> none  [local(): every_query = lax.all_gather(queries, 'sample', axis=0, tiled=True)]
    dot_general x14 -> x0, matrix products: 25.3 us -> none  [the longest x1 8.72 us: local(): jnp.einsum('ghk,lk->ghl', every_query, keys, preferred_element_type=jnp.f...]
  transfers between devices with their start and end apart: 4 -> 0, of which waited for: 4 -> 0; matrix products, arithmetic and copies ran while one was open for 2% -> 0% of each run, Pallas kernels for 0% -> 0%
where the time goes in v1:
time: 93.9 us; the launch traced here: 93.6 us
  Pallas kernels  90.2 us (96%)
  local copies, waits for them, and re-layouts  2.75 us (3%)
    pallas_call x1, Pallas kernels, local(): pl.pallas_call(kernel, out_shape=jax.ShapeDtypeStruct((8, 16, 128), BF16)...  90.2 us

profile of v1, /device:TPU:0, one launch (start us, length us, event | category | flops | bytes accessed | tf_op | source)
XLA Modules:
  0.0 93.6 jit_solution(6520075908874583379)
XLA Ops:
  0.7 1.3 %reshape.13.gain = bf16[1,7168]{1,0:T(2,128)(2,1)} reshape(bf16[7168]{0:T(1024)(128)(2,1)} %param.20) | data formatting | bytes 28672 | tf_op jit(solution)/shard_map/reshape | solution.py:638
  2.0 90.2 %layer.1 = bf16[8,16,128]{2,1,0:T(8,128)(2,1)} custom-call(bf16[64,576]{1,0:T(8,128)(2,1)} %bitcast.19, bf16[576,2048]{1,0:T(8,128)(2,1)} %bitcast.15, bf16[32,512,128]{2,1,0:T(8,128)(2,1)} %uv_in.1, bf16[256,7168]{1,0:T(8,128)(2,1)} %out_in.1, bf16[16,7168]{1,0:T(8,128)(2,1)} %bitcast.16, bf16[7168,256]{1,0:T(8,128)(2,1)} %bitcast.12, ...), custom_call_target="tpu_custom_call" | custom-call | tf_op jit(solution)/shard_map/layer/pallas_call | solution.py:617
  92.2 0.8 copy.16
  93.0 0.6 reshape.15
  (1 shorter events, 0.0 us)

commit v2 on v1

v2 whole, which is shorter than its diff:
```python
import functools
import jax
import jax.numpy as jnp
from jax import lax
from jax.experimental import pallas as pl
from jax.experimental.pallas import tpu as pltpu
from jax.sharding import PartitionSpec as P

MESH = pl.DeviceIdType.MESH
F32 = jnp.float32
BF16 = jnp.bfloat16
score_scale = 192.0 ** (-0.5)
log2e = 1.4426950408889634
route_scale = 2.827
norm_eps = 1e-06

COLS = 896
PIECES = ((384, 384, "xzy"), (384, 256, "yxz"), (256, 256, "zyx"))


def nt(a, b):
    return lax.dot_general(a, b, (((1,), (1,)), ((), ())), preferred_element_type=F32)


def mm(a, b):
    return jnp.dot(a, b, preferred_element_type=F32)


class Links:
    def __init__(self, send_sem, recv_sem, anyone):
        self.send_sem, self.recv_sem, self.anyone = send_sem, recv_sem, anyone
        self.sent, self.taken = [], 0

    def slots(self, n=1):
        self.taken += n
        return self.taken - n

    def send(self, src, dst, slot, device):
        copy = pltpu.make_async_remote_copy(
            src_ref=src,
            dst_ref=dst,
            send_sem=self.send_sem.at[len(self.sent)],
            recv_sem=self.recv_sem.at[slot],
            device_id=device,
            device_id_type=MESH,
        )
        copy.start()
        self.sent.append(copy)

    def arrived(self, dst, slot):
        pltpu.make_async_remote_copy(
            src_ref=dst,
            dst_ref=dst,
            send_sem=self.send_sem.at[0],
            recv_sem=self.recv_sem.at[slot],
            device_id=self.anyone,
            device_id_type=MESH,
        ).wait_recv()

    def finish(self):
        for copy in self.sent:
            copy.wait_send()


def kernel(
    q_in,
    cache_in,
    uv_in,
    out_in,
    router_in,
    gate_in,
    up_in,
    down_in,
    new_keys,
    residual,
    gain,
    ids,
    accept,
    assign,
    result,
    kc,
    wuv,
    wout,
    wgate,
    wup,
    wdown,
    rpad,
    qbuf,
    kn,
    obuf,
    vsend,
    vrecv,
    asend,
    arecv,
    hbuf,
    xa,
    xb,
    xc,
    pa,
    pb,
    pc,
    r1a,
    r1b,
    r1c,
    r2a,
    r2b,
    r2c,
    r3a,
    r3b,
    r3c,
    f1,
    f2,
    fsend,
    frecv,
    gf,
    load_sem,
    send_sem,
    recv_sem,
):
    p = lax.axis_index("prompt")
    s = lax.axis_index("sample")
    x, zh = p // 2, p % 2
    y, zl, k = s // 4, (s // 2) % 2, s % 2
    z = zh * 2 + zl
    chip = y * 2 + zl
    at = {"x": x, "y": y, "z": z}

    def device(x, y, z, k):
        return (x * 2 + z // 2, y * 4 + (z % 2) * 2 + k)

    def peer(axis, step):
        there = dict(at)
        there[axis] = (at[axis] + step) % 4
        return device(there["x"], there["y"], there["z"], k)

    def member(t):
        return (p, t)

    other = (p, y * 4 + zl * 2 + (1 - k))
    across = (p, y * 4 + (1 - zl) * 2 + k)

    first_column = pl.multiple_of(chip * COLS, 128)
    own_heads = pl.ds(pl.multiple_of(k * 16, 16), 16)
    own_units = pl.ds(pl.multiple_of(k * 256, 256), 256)
    loads = [
        pltpu.make_async_copy(src, dst, load_sem.at[n])
        for n, (src, dst) in enumerate(
            (
                (q_in.at[:, own_heads], qbuf.at[s]),
                (cache_in, kc.at[k]),
                (uv_in.at[own_heads], wuv),
                (out_in, wout),
                (router_in.at[:, pl.ds(first_column, COLS)], rpad.at[pl.ds(0, 16)]),
                (gate_in, wgate.at[k]),
                (up_in, wup.at[k]),
                (down_in, wdown.at[own_units]),
            )
        )
    ]
    for n in (0, 1, 2):
        loads[n].start()

    barrier = pltpu.get_barrier_semaphore()
    partners = [member((s + r) % 16) for r in range(1, 16)]
    partners += [peer("x", r) for r in (1, 2, 3)]
    partners += [device(x, y, (1 - zh) * 2 + r, k) for r in (0, 1)]
    for there in partners:
        pl.semaphore_signal(barrier, inc=1, device_id=there, device_id_type=MESH)
    pl.semaphore_wait(barrier, len(partners))

    links = Links(send_sem, recv_sem, other)
    send, arrived, slots = links.send, links.arrived, links.slots

    q_slot = slots(16)
    k_slot = slots(2)
    for dy in (0, 1, 3, 2):
        for dz in (0, 1):
            for dk in (1, 0):
                if (dy, dz, dk) == (0, 0, 0):
                    continue
                kk = (k + dk) % 2
                t = ((y + dy) % 4) * 4 + ((zl + dz) % 2) * 2 + kk
                heads = pl.ds(pl.multiple_of(kk * 16, 16), 16)
                send(q_in.at[:, heads], qbuf.at[s], q_slot + s, member(t))
        if dy == 0:
            send(cache_in, kc.at[k], k_slot, other)

    fresh = new_keys[...].astype(F32)
    row = lax.broadcasted_iota(jnp.int32, (16, 576), 0)
    kn[own_heads] = jnp.where(
        row == 0, fresh[0:1, :], jnp.where(row == 1, fresh[1:2, :], 0.0)
    ).astype(BF16)
    send(kn.at[own_heads], kn.at[own_heads], k_slot + 1, other)
    kn[pl.ds(32, 96)] = jnp.zeros((96, 576), BF16)
    rpad[pl.ds(16, 112)] = jnp.zeros((112, COLS), BF16)

    to_log2 = score_scale * log2e

    def attend(ya, yb, own):
        for yy in (ya, yb):
            for n in range(4):
                t = yy * 4 + n
                if own and yy is y:
                    t = y * 4 + (zl * 2 + k + n) % 4
                    if n == 0:
                        continue
                arrived(qbuf.at[t], q_slot + t)
        q = jnp.concatenate(
            [qbuf[pl.ds(yy * 4, 4)].reshape(128, 576) for yy in (ya, yb)], axis=0
        )
        scores = [mm(q, kc[n]) * to_log2 for n in range(2)]
        peaks = [jnp.max(part, axis=1, keepdims=True) for part in scores]
        peak = jnp.maximum(peaks[0], peaks[1])
        if own:
            row = lax.broadcasted_iota(jnp.int32, (256, 128), 0) - zl * 64
            column = lax.broadcasted_iota(jnp.int32, (256, 128), 1)
            seen = (
                (row >= 0)
                & (row < 64)
                & ((column >> 4) == (row >> 5))
                & ((column & 15) <= ((row >> 4) & 1))
            )
            own_scores = jnp.where(seen, nt(q, kn[...]) * to_log2, -jnp.inf)
            peak = jnp.maximum(peak, jnp.max(own_scores, axis=1, keepdims=True))
        denom = jnp.zeros((256, 1), F32)
        latent = jnp.zeros((256, 512), F32)
        for n in range(2):
            weights = jnp.exp2(scores[n] - peak)
            denom = denom + jnp.sum(weights, axis=1, keepdims=True)
            latent = latent + nt(weights.astype(BF16), kc[n, pl.ds(0, 512), :])
        if own:
            own_weights = jnp.exp2(own_scores - peak)
            denom = denom + jnp.sum(own_weights, axis=1, keepdims=True)
            latent = latent + mm(own_weights.astype(BF16), kn[:, pl.ds(0, 512)])
        latent = latent / denom
        level = jnp.broadcast_to(peak + jnp.log2(denom), (256, 128))
        for i, yy in enumerate((ya, yb)):
            at_rows = pl.ds(pl.multiple_of(yy * 128, 128), 128)
            for n in range(4):
                obuf[n, at_rows, :] = latent[i * 128 : i * 128 + 128, n * 128 : n * 128 + 128]
            obuf[4, at_rows, :] = level[i * 128 : i * 128 + 128]

    loads[0].wait()
    loads[1].wait()
    arrived(kn.at[pl.ds(pl.multiple_of(16 - k * 16, 16), 16)], k_slot + 1)
    arrived(kc.at[1 - k], k_slot)
    for n in (3, 4, 5, 6, 7):
        loads[n].start()
    w_slot = slots(3)
    send(gate_in, wgate.at[k], w_slot, other)
    send(up_in, wup.at[k], w_slot + 1, other)
    send(down_in, wdown.at[own_units], w_slot + 2, other)
    attend(y, (y + 1) % 4, True)
    attend((y + 3) % 4, (y + 2) % 4, False)

    lane32 = lax.broadcasted_iota(jnp.int32, (32, 128), 1)
    v_slot = slots(8)
    own_share = (s // 8) == k
    loads[2].wait()
    own_send = None
    for r in (4, 5, 3, 6, 2, 7, 1, 0):
        local_owner = (s + r) % 8
        owner = k * 8 + local_owner
        stats = jnp.zeros((32, 128), F32)
        halves = []
        for j in range(2):
            head = local_owner * 2 + j
            mine = [obuf[n, pl.ds(head, 32, stride=16), :] for n in range(5)]
            latent = jnp.concatenate(mine[:4], axis=1).astype(BF16)
            halves.append(mm(latent, wuv[head]).astype(BF16))
            level = mine[4]
            high = level.astype(BF16).astype(F32)
            middle = (level - high).astype(BF16).astype(F32)
            low = level - high - middle
            stats = jnp.where(lane32 == j * 64, high, stats)
            stats = jnp.where(lane32 == j * 64 + 1, middle, stats)
            stats = jnp.where(lane32 == j * 64 + 2, low, stats)
        vsend[r] = jnp.concatenate(halves + [stats.astype(BF16)], axis=1)
        if r:
            send(vsend.at[r], vrecv.at[chip], v_slot + chip, member(owner))
        else:
            own_send = pltpu.make_async_remote_copy(
                src_ref=vsend.at[r],
                dst_ref=vrecv.at[chip],
                send_sem=load_sem.at[8],
                recv_sem=recv_sem.at[v_slot + chip],
                device_id=member(owner),
                device_id_type=MESH,
            )

            @pl.when(own_share)
            def _():
                vrecv[chip] = vsend[0]

            @pl.when(jnp.logical_not(own_share))
            def _():
                own_send.start()

    row32 = lax.broadcasted_iota(jnp.int32, (32, 128), 0)
    own_ids = ids[...]
    targets = assign[...]
    places = ((targets >> 1) & 1) * 16 + (targets >> 2) * 2 + (targets & 1)
    move = (lax.broadcasted_iota(jnp.int32, (32, 32), 0) == places).astype(BF16)
    spots = lax.broadcasted_iota(jnp.int32, (1, 32), 1)

    facts = jnp.zeros((32, 128), F32)
    own_places = []
    for t in range(2):
        mark = jnp.zeros((32, 128), F32)
        for j in range(8):
            mark = mark + jnp.where(lane32 == own_ids[t : t + 1, j : j + 1] + 48, 0.125, 0.0)
        keep = jnp.ones((1, 1), F32) if t == 0 else accept[...].astype(F32)
        mark = mark + jnp.where(lane32 == 65, keep, 0.0)
        place = jnp.sum(jnp.where(spots == 2 * s + t, places, 0), axis=1, keepdims=True)
        own_places.append(place)
        facts = jnp.where(row32 == place, mark, facts)
    facts = facts.astype(BF16)

    for r in range(1, 8):
        c = (chip + r) % 8
        arrived(vrecv.at[c], v_slot + c)

    @pl.when(jnp.logical_not(own_share))
    def _():
        arrived(vrecv.at[chip], v_slot + chip)
        own_send.wait_send()

    lane3 = lax.broadcasted_iota(jnp.int32, (8, 32, 128), 2)
    got = vrecv[:, :, pl.ds(256, 128)].astype(F32)
    values = []
    for j in range(2):
        inside = (lane3 >= j * 64) & (lane3 < j * 64 + 3)
        level = jnp.sum(jnp.where(inside, got, 0.0), axis=2, keepdims=True)
        share = jnp.exp2(level - jnp.max(level, axis=0, keepdims=True))
        total = jnp.sum(share, axis=0)
        heard = vrecv[:, :, pl.ds(j * 128, 128)].astype(F32)
        values.append(jnp.sum(heard * share, axis=0) / total)
    values = jnp.concatenate(values, axis=1).astype(BF16)
    values = mm(move, values).astype(BF16)

    a_slot = slots(16)
    loads[3].wait()
    row_wide = lax.broadcasted_iota(jnp.int32, (32, COLS), 0)
    for dy in (2, 1, 3, 0):
        for dz in (1, 0):
            c = ((y + dy) % 4) * 2 + (zl + dz) % 2
            columns = pl.ds(pl.multiple_of(c * COLS, 128), COLS)
            part = mm(values, wout[:, columns])
            rest = residual[:, columns].astype(F32)
            part = part + jnp.where(
                row_wide == own_places[0],
                rest[0:1, :],
                jnp.where(row_wide == own_places[1], rest[1:2, :], 0.0),
            )
            part = jnp.concatenate([part.astype(BF16), facts], axis=1)
            n = (dy * 2 + dz) * 2
            asend[n] = part[:16]
            asend[n + 1] = part[16:]
            far = (dy, dz) != (0, 0)
            if far:
                for kk in range(2):
                    send(asend.at[n + kk], arecv.at[s], a_slot + s, member(c * 2 + kk))
            else:
                send(asend.at[n + 1 - k], arecv.at[s], a_slot + s, other)
                arecv[s] = asend[n + k]
    for r in range(1, 16):
        source = (s + r) % 16
        arrived(arecv.at[source], a_slot + source)
    total = jnp.sum(arecv[...].astype(F32), axis=0)
    hidden = total[:, :COLS].astype(BF16).astype(F32)
    facts = total[:, COLS:]
    note_lane = lax.broadcasted_iota(jnp.int32, (16, 128), 1)
    keep = jnp.sum(jnp.where(note_lane == 65, facts, 0.0), axis=1, keepdims=True)

    hbuf[...] = hidden

    loads[4].wait()
    gf[...] = gain[...].astype(F32)
    own_gain = jnp.concatenate([gf[pl.ds(chip * 7 + j, 1), :] for j in range(7)], axis=1)
    block = (hidden * own_gain).astype(BF16)
    squares = jnp.sum(hidden * hidden, axis=1, keepdims=True)
    squares_high = squares.astype(BF16).astype(F32)
    logits = nt(block, rpad[...])
    logits_high = logits.astype(BF16).astype(F32)
    note = logits_high + pltpu.roll(logits - logits_high, 16, 1) + facts
    note = note + jnp.where(note_lane == 32, squares_high, 0.0)
    note = note + jnp.where(note_lane == 33, squares - squares_high, 0.0)
    tail = jnp.concatenate([block[:, 768:], note.astype(BF16)], axis=1)
    gathered = (xa, xb, xc)
    for buf, (w, _, order), piece in zip(
        gathered, PIECES, (block[:, :384], block[:, 384:768], tail)
    ):
        c1, c2, c3 = (at[axis] for axis in order)
        buf[c3, c2, c1] = piece

    plan = []
    for buf, (w, _, order) in zip(gathered, PIECES):
        plan.append((buf, order, tuple(at[axis] for axis in order), slots(3), slots(3), slots(6)))
    for o in (2, 1, 3):
        for buf, order, (c1, c2, c3), s1, s2, s3 in plan:
            mine = buf.at[c3, c2, c1]
            send(mine, mine, s1 + o - 1, peer(order[0], o))
    for buf, order, (c1, c2, c3), s1, s2, s3 in plan:
        for o in (1, 3, 2):
            arrived(buf.at[c3, c2, (c1 + 4 - o) % 4], s1 + o - 1)
        mine = buf.at[c3, c2]
        for o in (2, 1, 3):
            send(mine, mine, s2 + o - 1, peer(order[1], o))
    for buf, order, (c1, c2, c3), s1, s2, s3 in plan:
        for o in (1, 3, 2):
            arrived(buf.at[c3, (c2 + 4 - o) % 4], s2 + o - 1)

    def half(buf, c3, h):
        return buf.at[c3, pl.ds(2 * h, 2)]

    for h, o in ((0, 1), (1, 3), (0, 3), (1, 1)):
        for buf, order, (c1, c2, c3), s1, s2, s3 in plan:
            mine = half(buf, c3, h)
            send(mine, mine, s3 + (0 if o == 1 else 2) + h, peer(order[2], o))

    def rows_of(n, yy, zz, columns):
        blocks = []
        for hh in range(2):
            for xx in range(4):
                c = {"x": xx, "y": yy, "z": hh * 2 + zz}
                c1, c2, c3 = (c[axis] for axis in PIECES[n][2])
                blocks.append(gathered[n][c3, c2, c1, :, columns])
        return jnp.concatenate(blocks, axis=0)

    parts = [[jnp.zeros((128, 256), F32) for _ in range(2)] for _ in range(2)]

    def multiply(n, yy, first, width):
        for zz in range(2):
            tokens = rows_of(n, yy, zz, pl.ds(0, width))
            at_rows = pl.ds(pl.multiple_of((yy * 2 + zz) * COLS + first, 128), width)
            for b in range(2):
                parts[b][0] = parts[b][0] + mm(tokens, wgate[b, at_rows, :])
                parts[b][1] = parts[b][1] + mm(tokens, wup[b, at_rows, :])

    loads[5].wait()
    loads[6].wait()
    arrived(wgate.at[1 - k], w_slot)
    arrived(wup.at[1 - k], w_slot + 1)
    multiply(0, y, 0, 384)
    for buf, order, (c1, c2, c3), s1, s2, s3 in plan:
        for c, h, n, o in (((c3 + 3) % 4, 0, 0, 1), ((c3 + 1) % 4, 1, 3, 3)):
            view = half(buf, c, h)
            arrived(view, s3 + n)
            send(view, view, s3 + 4 + h, peer(order[2], o))

    def rest(n, last):
        buf, order, (c1, c2, c3), s1, s2, s3 = plan[n]
        if last:
            arrived(half(buf, (c3 + 2) % 4, 0), s3 + 4)
            arrived(half(buf, (c3 + 2) % 4, 1), s3 + 5)
        else:
            arrived(half(buf, (c3 + 3) % 4, 1), s3 + 1)
            arrived(half(buf, (c3 + 1) % 4, 0), s3 + 2)

    rest(0, False)
    multiply(0, (y + 3) % 4, 0, 384)
    multiply(0, (y + 1) % 4, 0, 384)
    rest(0, True)
    multiply(0, (y + 2) % 4, 0, 384)
    rest(1, False)
    rest(1, True)
    for yy in range(4):
        multiply(1, yy, 384, 384)
    rest(2, False)
    rest(2, True)
    note = jnp.zeros((128, 128), F32)
    for yy in range(4):
        multiply(2, yy, 768, 128)
        for zz in range(2):
            note = note + rows_of(2, yy, zz, pl.ds(128, 128)).astype(F32)

    lane = lax.broadcasted_iota(jnp.int32, (128, 128), 1)

    def column_sum(inside):
        return jnp.sum(jnp.where(inside, note, 0.0), axis=1, keepdims=True)

    model_width = 8 * COLS
    scale = lax.rsqrt(column_sum((lane == 32) | (lane == 33)) / model_width + norm_eps)
    logits = (note + pltpu.roll(note, 112, 1)) * scale
    chosen = jnp.where(lane < 16, jax.nn.sigmoid(logits) * pltpu.roll(note, 80, 1), 0.0)
    expert = (p * 16 + s) // 8
    gate = jnp.sum(jnp.where(lane == expert, chosen, 0.0), axis=1, keepdims=True)
    gate = gate / jnp.sum(chosen, axis=1, keepdims=True) * route_scale
    act = [jax.nn.silu(g * scale) * (u * scale) * gate for g, u in parts]
    act = jnp.concatenate(act, axis=1).astype(BF16)

    loads[7].wait()
    arrived(wdown.at[pl.ds(pl.multiple_of(256 - k * 256, 256), 256)], w_slot + 2)
    partial = (pa, pb, pc)
    for yy in range(4):
        for zz in range(2):
            part = mm(act, wdown[:, pl.ds((yy * 2 + zz) * COLS, COLS)]).astype(BF16)
            start = 0
            for buf, (_, w, order) in zip(partial, PIECES):
                for hh in range(2):
                    for xx in range(4):
                        at_block = {"x": xx, "y": yy, "z": hh * 2 + zz}
                        c1, c2, c3 = (at_block[axis] for axis in order)
                        first = (hh * 4 + xx) * 16
                        buf[c3, c2, c1] = part[first : first + 16, start : start + w]
                start += w
    plan = []
    for n, (_, w, order) in enumerate(PIECES):
        bufs = (partial[n], (r1a, r1b, r1c)[n], (r2a, r2b, r2c)[n], (r3a, r3b, r3c)[n])
        plan.append((bufs, order, tuple(at[axis] for axis in order), slots(6), slots(3), slots(3)))

    def add_to(ref, *terms):
        total = ref[...].astype(F32)
        for term in terms:
            total = total + term[...].astype(F32)
        ref[...] = total.astype(BF16)

    for n, (step, h, o) in enumerate(((2, 0, 1), (2, 1, 3), (1, 1, 1), (3, 0, 3))):
        for (part, r1, r2, r3), order, (c1, c2, c3), s1, s2, s3 in plan:
            send(half(part, (c3 + step) % 4, h), r1.at[n], s1 + n, peer(order[2], o))
    for n, (step, h, o) in enumerate(((1, 0, 1), (3, 1, 3))):
        for (part, r1, r2, r3), order, (c1, c2, c3), s1, s2, s3 in plan:
            view = half(part, (c3 + step) % 4, h)
            arrived(r1.at[n], s1 + n)
            add_to(view, r1.at[n])
            send(view, r1.at[n + 4], s1 + n + 4, peer(order[2], o))
    for (part, r1, r2, r3), order, (c1, c2, c3), s1, s2, s3 in plan:
        for n in (2, 3, 4, 5):
            arrived(r1.at[n], s1 + n)
        add_to(half(part, c3, 0), r1.at[3], r1.at[4])
        add_to(half(part, c3, 1), r1.at[2], r1.at[5])
        for o in (2, 1, 3):
            send(part.at[c3, (c2 + o) % 4], r2.at[o - 1], s2 + o - 1, peer(order[1], o))
    for (part, r1, r2, r3), order, (c1, c2, c3), s1, s2, s3 in plan:
        for o in (1, 2, 3):
            arrived(r2.at[o - 1], s2 + o - 1)
        add_to(part.at[c3, c2], r2.at[0], r2.at[1], r2.at[2])
        for o in (2, 1, 3):
            send(part.at[c3, c2, (c1 + o) % 4], r3.at[o - 1], s3 + o - 1, peer(order[0], o))
    sums = []
    for (part, r1, r2, r3), order, (c1, c2, c3), s1, s2, s3 in plan:
        for o in (1, 2, 3):
            arrived(r3.at[o - 1], s3 + o - 1)
        sums.append(part[c3, c2, c1].astype(F32) + jnp.sum(r3[...].astype(F32), axis=0))
    final = (jnp.concatenate(sums, axis=1) + hbuf[...]) * keep
    for j in range(7):
        f1[j] = final[:, j * 128 : (j + 1) * 128]

    f2[...] = jnp.zeros_like(f2)
    for t in range(2):
        for j in range(7):
            f2[pl.ds(t * 7 + j, 8, stride=16), :] = f1[j, pl.ds(t, 8, stride=2), :]
    fsend[...] = f2[...].reshape(8, 16, 128).astype(BF16)
    f_slot = slots(8)
    for r in range(1, 8):
        c = (chip + r) % 8
        send(fsend.at[c], frecv.at[chip], f_slot + chip, member(c * 2 + k))
    frecv[chip] = fsend[chip]
    for r in range(1, 8):
        c = (chip + r) % 8
        arrived(frecv.at[c], f_slot + c)
    f2[...] = frecv[...].reshape(128, 128).astype(F32)
    rows = [f2[pl.ds(c * 16 + j, 2, stride=7), :] for c in range(8) for j in range(7)]
    result[...] = jnp.concatenate(rows, axis=1).astype(BF16)
    links.finish()


def local(
    queries,
    new_keys,
    cache,
    residual,
    w_uv,
    w_out,
    norm_gain,
    router,
    expert_ids,
    w_gate,
    w_up,
    w_down,
    accept,
    assign,
):
    positions = cache.shape[1]
    whole = pl.BlockSpec(memory_space=pltpu.VMEM)
    left = pl.BlockSpec(memory_space=pl.ANY)
    scratch = [
        pltpu.VMEM((2, 576, positions), BF16),
        pltpu.VMEM((16, 512, 128), BF16),
        pltpu.VMEM((256, 7168), BF16),
        pltpu.VMEM((2, 7168, 256), BF16),
        pltpu.VMEM((2, 7168, 256), BF16),
        pltpu.VMEM((512, 7168), BF16),
        pltpu.VMEM((128, COLS), BF16),
        pltpu.VMEM((16, 2, 16, 576), BF16),
        pltpu.VMEM((128, 576), BF16),
        pltpu.VMEM((5, 512, 128), F32),
        pltpu.VMEM((8, 32, 384), BF16),
        pltpu.VMEM((8, 32, 384), BF16),
        pltpu.VMEM((16, 16, COLS + 128), BF16),
        pltpu.VMEM((16, 16, COLS + 128), BF16),
        pltpu.VMEM((16, COLS), F32),
    ]
    scratch += [pltpu.VMEM((4, 4, 4, 16, w), BF16) for w, _, _ in PIECES]
    scratch += [pltpu.VMEM((4, 4, 4, 16, w), BF16) for _, w, _ in PIECES]
    scratch += [pltpu.VMEM((6, 2, 4, 16, w), BF16) for _, w, _ in PIECES]
    scratch += [pltpu.VMEM((3, 4, 16, w), BF16) for _, w, _ in PIECES]
    scratch += [pltpu.VMEM((3, 16, w), BF16) for _, w, _ in PIECES]
    scratch += [
        pltpu.VMEM((7, 16, 128), F32),
        pltpu.VMEM((128, 128), F32),
        pltpu.VMEM((8, 16, 128), BF16),
        pltpu.VMEM((8, 16, 128), BF16),
        pltpu.VMEM((56, 128), F32),
        pltpu.SemaphoreType.DMA((9,)),
        pltpu.SemaphoreType.DMA((192,)),
        pltpu.SemaphoreType.DMA((192,)),
    ]
    rows = pl.pallas_call(
        kernel,
        out_shape=jax.ShapeDtypeStruct((2, 7168), BF16),
        in_specs=[left] * 8 + [whole] * 6,
        out_specs=whole,
        scratch_shapes=scratch,
        compiler_params=pltpu.CompilerParams(
            collective_id=0, has_side_effects=True, vmem_limit_bytes=60 * 1024 * 1024
        ),
        name="layer",
    )(
        queries,
        cache[0].T,
        w_uv,
        w_out,
        router.T,
        w_gate[0],
        w_up[0],
        w_down[0],
        new_keys,
        residual,
        norm_gain.reshape(56, 128),
        expert_ids,
        accept,
        assign,
    )
    return rows


def solution(mesh):
    placed = (
        P(("prompt", "sample"), None, None),
        P(("prompt", "sample"), None),
        P("prompt", "sample", None),
        P(("prompt", "sample"), None),
        P(),
        P("sample", None),
        P(),
        P(),
        P(("prompt", "sample"), None),
        P(("prompt", "sample"), None, None),
        P(("prompt", "sample"), None, None),
        P(("prompt", "sample"), None, None),
        P("prompt", "sample"),
        P("prompt", None),
    )
    return jax.shard_map(
        local, mesh=mesh, in_specs=placed, out_specs=P(("prompt", "sample"), None), check_vma=False
    )
```

time: 93.9 us -> 85.2 us (0.907)
  Pallas kernels: 90.2 us -> 83 us
  local copies, waits for them, and re-layouts: 2.75 us -> 1.38 us
    pallas_call x1, Pallas kernels: 90.2 us -> 83 us  [local(): pl.pallas_call(kernel, out_shape=jax.ShapeDtypeStruct((2, 7168), BF16), i...]
    reshape x2 -> x0, local copies, waits for them, and re-layouts: 1.97 us -> none  [the longest x1 1.34 us: local(): norm_gain.reshape(1, 7168)]
    unnamed x0 -> x1, local copies, waits for them, and re-layouts: none -> 1.38 us
where the time goes in v2:
time: 85.2 us; the launch traced here: 85 us
  Pallas kernels  83 us (97%)
  local copies, waits for them, and re-layouts  1.38 us (2%)
    pallas_call x1, Pallas kernels, local(): pl.pallas_call(kernel, out_shape=jax.ShapeDtypeStruct((2, 7168), BF16), i...  83 us

profile of v2, /device:TPU:0, one launch (start us, length us, event | category | flops | bytes accessed | tf_op | source)
XLA Modules:
  0.0 85.0 jit_solution(11838167921280663070)
XLA Ops:
  0.7 83.0 %layer.1 = bf16[2,7168]{1,0:T(2,128)(2,1)} custom-call(bf16[2,32,576]{2,1,0:T(8,128)(2,1)} %q_in.1, bf16[576,2048]{1,0:T(8,128)(2,1)} %bitcast.11, bf16[32,512,128]{2,1,0:T(8,128)(2,1)} %uv_in.1, bf16[256,7168]{1,0:T(8,128)(2,1)} %out_in.1, bf16[16,7168]{1,0:T(8,128)(2,1)} %bitcast.12, bf16[7168,256]{1,0:T(8,128)(2,1)} %bitcast.8, ...), custom_call_target="tpu_custom_call" | custom-call | tf_op jit(solution)/shard_map/layer/pallas_call | solution.py:619
  83.6 1.4 %copy.17 = bf16[2,7168]{1,0:T(2,128)(2,1)} copy(bf16[2,7168]{1,0:T(2,128)(2,1)} %layer.1) | data formatting | bytes 57344

commit v3 on v2

--- a/solution.py
+++ b/solution.py
@@ -92,7 +92,7 @@
     vrecv,
     asend,
     arecv,
-    hbuf,
+    stage,
     xa,
     xb,
     xc,
@@ -105,14 +105,12 @@
     r2a,
     r2b,
     r2c,
-    r3a,
-    r3b,
-    r3c,
     f1,
     f2,
     fsend,
     frecv,
     gf,
+    extra,
     load_sem,
     send_sem,
     recv_sem,
@@ -133,6 +131,12 @@
         there[axis] = (at[axis] + step) % 4
         return device(there["x"], there["y"], there["z"], k)
 
+    def beside(order, o1, o2):
+        there = dict(at)
+        there[order[0]] = (at[order[0]] + o1) % 4
+        there[order[1]] = (at[order[1]] + o2) % 4
+        return device(there["x"], there["y"], there["z"], k)
+
     def member(t):
         return (p, t)
 
@@ -149,7 +153,7 @@
                 (q_in.at[:, own_heads], qbuf.at[s]),
                 (cache_in, kc.at[k]),
                 (uv_in.at[own_heads], wuv),
-                (out_in, wout),
+                (out_in, wout.at[own_units]),
                 (router_in.at[:, pl.ds(first_column, COLS)], rpad.at[pl.ds(0, 16)]),
                 (gate_in, wgate.at[k]),
                 (up_in, wup.at[k]),
@@ -162,8 +166,15 @@
 
     barrier = pltpu.get_barrier_semaphore()
     partners = [member((s + r) % 16) for r in range(1, 16)]
-    partners += [peer("x", r) for r in (1, 2, 3)]
-    partners += [device(x, y, (1 - zh) * 2 + r, k) for r in (0, 1)]
+    planes = [(dx, dy, dz) for dx in range(4) for dy in range(4) for dz in range(4) if 0 in (dx, dy, dz)]
+    for dx, dy, dz in planes:
+        if dx:
+            partners.append(device((x + dx) % 4, (y + dy) % 4, (z + dz) % 4, k))
+        elif dz in (1, 3):
+            if dz == 1:
+                partners.append(device(x, (y + dy) % 4, (1 - zh) * 2, k))
+            else:
+                partners.append(device(x, (y + dy) % 4, (1 - zh) * 2 + 1, k))
     for there in partners:
         pl.semaphore_signal(barrier, inc=1, device_id=there, device_id_type=MESH)
     pl.semaphore_wait(barrier, len(partners))
@@ -173,7 +184,7 @@
 
     q_slot = slots(16)
     k_slot = slots(2)
-    for dy in (0, 1, 3, 2):
+    for dy in (0, 3, 1, 2):
         for dz in (0, 1):
             for dk in (1, 0):
                 if (dy, dz, dk) == (0, 0, 0):
@@ -193,6 +204,26 @@
     send(kn.at[own_heads], kn.at[own_heads], k_slot + 1, other)
     kn[pl.ds(32, 96)] = jnp.zeros((96, 576), BF16)
     rpad[pl.ds(16, 112)] = jnp.zeros((112, COLS), BF16)
+
+    extra_row = lax.broadcasted_iota(jnp.int32, (16, 7168), 0)
+    rest = residual[...].astype(F32)
+    extra[k, :, pl.ds(0, 7168)] = jnp.where(
+        extra_row == 0, rest[0:1, :], jnp.where(extra_row == 1, rest[1:2, :], 0.0)
+    ).astype(BF16)
+    note_row = lax.broadcasted_iota(jnp.int32, (16, 128), 0)
+    note_lane = lax.broadcasted_iota(jnp.int32, (16, 128), 1)
+    own_ids = ids[...]
+    facts = jnp.zeros((16, 128), F32)
+    for t in range(2):
+        mark = jnp.zeros((16, 128), F32)
+        for j in range(8):
+            mark = mark + jnp.where(note_lane == own_ids[t : t + 1, j : j + 1] + 48, 0.125, 0.0)
+        keep = jnp.ones((1, 1), F32) if t == 0 else accept[...].astype(F32)
+        mark = mark + jnp.where(note_lane == 65, keep, 0.0)
+        facts = jnp.where(note_row == t, mark, facts)
+    extra[k, :, pl.ds(7168, 128)] = facts.astype(BF16)
+    e_slot = slots(1)
+    send(extra.at[k], extra.at[k], e_slot, other)
 
     to_log2 = score_scale * log2e
 
@@ -246,75 +277,61 @@
     arrived(kc.at[1 - k], k_slot)
     for n in (3, 4, 5, 6, 7):
         loads[n].start()
-    w_slot = slots(3)
+    w_slot = slots(4)
+    send(out_in, wout.at[own_units], w_slot + 3, other)
     send(gate_in, wgate.at[k], w_slot, other)
     send(up_in, wup.at[k], w_slot + 1, other)
     send(down_in, wdown.at[own_units], w_slot + 2, other)
     attend(y, (y + 1) % 4, True)
     attend((y + 3) % 4, (y + 2) % 4, False)
 
+    targets = assign[...]
+    places = ((targets >> 1) & 1) * 16 + (targets >> 2) * 2 + (targets & 1)
+    move = (lax.broadcasted_iota(jnp.int32, (32, 32), 0) == places).astype(BF16)
+    spots = lax.broadcasted_iota(jnp.int32, (1, 32), 1)
+
     lane32 = lax.broadcasted_iota(jnp.int32, (32, 128), 1)
     v_slot = slots(8)
-    own_share = (s // 8) == k
+    own_share = (chip // 4) == k
     loads[2].wait()
-    own_send = None
-    for r in (4, 5, 3, 6, 2, 7, 1, 0):
-        local_owner = (s + r) % 8
-        owner = k * 8 + local_owner
+    for r in (2, 1, 3, 0):
+        local_chip = (chip + r) % 4
+        there = k * 4 + local_chip
         stats = jnp.zeros((32, 128), F32)
-        halves = []
-        for j in range(2):
-            head = local_owner * 2 + j
+        shares = []
+        for j in range(4):
+            head = local_chip * 4 + j
             mine = [obuf[n, pl.ds(head, 32, stride=16), :] for n in range(5)]
             latent = jnp.concatenate(mine[:4], axis=1).astype(BF16)
-            halves.append(mm(latent, wuv[head]).astype(BF16))
+            shares.append(mm(latent, wuv[head]).astype(BF16))
             level = mine[4]
             high = level.astype(BF16).astype(F32)
             middle = (level - high).astype(BF16).astype(F32)
             low = level - high - middle
-            stats = jnp.where(lane32 == j * 64, high, stats)
-            stats = jnp.where(lane32 == j * 64 + 1, middle, stats)
-            stats = jnp.where(lane32 == j * 64 + 2, low, stats)
-        vsend[r] = jnp.concatenate(halves + [stats.astype(BF16)], axis=1)
+            stats = jnp.where(lane32 == j * 32, high, stats)
+            stats = jnp.where(lane32 == j * 32 + 1, middle, stats)
+            stats = jnp.where(lane32 == j * 32 + 2, low, stats)
+        message = jnp.concatenate(shares + [stats.astype(BF16)], axis=1)
+        vsend[r] = mm(move, message).astype(BF16).reshape(2, 16, 640)
+        send(vsend.at[r, 1 - k], vrecv.at[chip], v_slot + chip, member(there * 2 + 1 - k))
         if r:
-            send(vsend.at[r], vrecv.at[chip], v_slot + chip, member(owner))
-        else:
-            own_send = pltpu.make_async_remote_copy(
-                src_ref=vsend.at[r],
-                dst_ref=vrecv.at[chip],
-                send_sem=load_sem.at[8],
-                recv_sem=recv_sem.at[v_slot + chip],
-                device_id=member(owner),
-                device_id_type=MESH,
-            )
-
-            @pl.when(own_share)
-            def _():
-                vrecv[chip] = vsend[0]
-
-            @pl.when(jnp.logical_not(own_share))
-            def _():
-                own_send.start()
-
-    row32 = lax.broadcasted_iota(jnp.int32, (32, 128), 0)
-    own_ids = ids[...]
-    targets = assign[...]
-    places = ((targets >> 1) & 1) * 16 + (targets >> 2) * 2 + (targets & 1)
-    move = (lax.broadcasted_iota(jnp.int32, (32, 32), 0) == places).astype(BF16)
-    spots = lax.broadcasted_iota(jnp.int32, (1, 32), 1)
-
-    facts = jnp.zeros((32, 128), F32)
-    own_places = []
-    for t in range(2):
-        mark = jnp.zeros((32, 128), F32)
-        for j in range(8):
-            mark = mark + jnp.where(lane32 == own_ids[t : t + 1, j : j + 1] + 48, 0.125, 0.0)
-        keep = jnp.ones((1, 1), F32) if t == 0 else accept[...].astype(F32)
-        mark = mark + jnp.where(lane32 == 65, keep, 0.0)
-        place = jnp.sum(jnp.where(spots == 2 * s + t, places, 0), axis=1, keepdims=True)
-        own_places.append(place)
-        facts = jnp.where(row32 == place, mark, facts)
-    facts = facts.astype(BF16)
+            send(vsend.at[r, k], vrecv.at[chip], v_slot + chip, member(there * 2 + k))
+    own_send = pltpu.make_async_remote_copy(
+        src_ref=vsend.at[0, k],
+        dst_ref=vrecv.at[chip],
+        send_sem=load_sem.at[8],
+        recv_sem=recv_sem.at[v_slot + chip],
+        device_id=member((k * 4 + chip % 4) * 2 + k),
+        device_id_type=MESH,
+    )
+
+    @pl.when(own_share)
+    def _():
+        vrecv[chip] = vsend[0, k]
+
+    @pl.when(jnp.logical_not(own_share))
+    def _():
+        own_send.start()
 
     for r in range(1, 8):
         c = (chip + r) % 8
@@ -325,54 +342,58 @@
         arrived(vrecv.at[chip], v_slot + chip)
         own_send.wait_send()
 
-    lane3 = lax.broadcasted_iota(jnp.int32, (8, 32, 128), 2)
-    got = vrecv[:, :, pl.ds(256, 128)].astype(F32)
+    lane3 = lax.broadcasted_iota(jnp.int32, (8, 16, 128), 2)
+    got = vrecv[:, :, pl.ds(512, 128)].astype(F32)
     values = []
-    for j in range(2):
-        inside = (lane3 >= j * 64) & (lane3 < j * 64 + 3)
+    for j in range(4):
+        inside = (lane3 >= j * 32) & (lane3 < j * 32 + 3)
         level = jnp.sum(jnp.where(inside, got, 0.0), axis=2, keepdims=True)
         share = jnp.exp2(level - jnp.max(level, axis=0, keepdims=True))
         total = jnp.sum(share, axis=0)
         heard = vrecv[:, :, pl.ds(j * 128, 128)].astype(F32)
         values.append(jnp.sum(heard * share, axis=0) / total)
     values = jnp.concatenate(values, axis=1).astype(BF16)
-    values = mm(move, values).astype(BF16)
-
-    a_slot = slots(16)
+
+    a_slot = slots(8)
     loads[3].wait()
-    row_wide = lax.broadcasted_iota(jnp.int32, (32, COLS), 0)
+    arrived(wout.at[pl.ds(pl.multiple_of(256 - k * 256, 256), 256)], w_slot + 3)
+    arrived(extra.at[1 - k], e_slot)
+    row_wide = lax.broadcasted_iota(jnp.int32, (16, COLS), 0)
+    own_rows = []
+    for kk in range(2):
+        for t in range(2):
+            spot = (chip * 2 + kk) * 2 + t
+            place = jnp.sum(jnp.where(spots == spot, places, 0), axis=1, keepdims=True)
+            own_rows.append((kk, t, place - k * 16))
+
+    def with_extra(value, rows, columns):
+        for kk in range(2):
+            rest = extra[kk, :, columns].astype(F32)
+            for other_kk, t, place in own_rows:
+                if other_kk == kk:
+                    value = value + jnp.where(rows == place, rest[t : t + 1, :], 0.0)
+        return value
+
+    facts = with_extra(jnp.zeros((16, 128), F32), note_row, pl.ds(7168, 128)).astype(BF16)
     for dy in (2, 1, 3, 0):
         for dz in (1, 0):
             c = ((y + dy) % 4) * 2 + (zl + dz) % 2
             columns = pl.ds(pl.multiple_of(c * COLS, 128), COLS)
-            part = mm(values, wout[:, columns])
-            rest = residual[:, columns].astype(F32)
-            part = part + jnp.where(
-                row_wide == own_places[0],
-                rest[0:1, :],
-                jnp.where(row_wide == own_places[1], rest[1:2, :], 0.0),
-            )
+            part = with_extra(mm(values, wout[:, columns]), row_wide, columns)
             part = jnp.concatenate([part.astype(BF16), facts], axis=1)
-            n = (dy * 2 + dz) * 2
-            asend[n] = part[:16]
-            asend[n + 1] = part[16:]
-            far = (dy, dz) != (0, 0)
-            if far:
-                for kk in range(2):
-                    send(asend.at[n + kk], arecv.at[s], a_slot + s, member(c * 2 + kk))
+            if (dy, dz) == (0, 0):
+                arecv[chip] = part
             else:
-                send(asend.at[n + 1 - k], arecv.at[s], a_slot + s, other)
-                arecv[s] = asend[n + k]
-    for r in range(1, 16):
-        source = (s + r) % 16
-        arrived(arecv.at[source], a_slot + source)
+                n = dy * 2 + dz
+                asend[n] = part
+                send(asend.at[n], arecv.at[chip], a_slot + chip, member(c * 2 + k))
+    for r in range(1, 8):
+        c = (chip + r) % 8
+        arrived(arecv.at[c], a_slot + c)
     total = jnp.sum(arecv[...].astype(F32), axis=0)
     hidden = total[:, :COLS].astype(BF16).astype(F32)
     facts = total[:, COLS:]
-    note_lane = lax.broadcasted_iota(jnp.int32, (16, 128), 1)
     keep = jnp.sum(jnp.where(note_lane == 65, facts, 0.0), axis=1, keepdims=True)
-
-    hbuf[...] = hidden
 
     loads[4].wait()
     gf[...] = gain[...].astype(F32)
@@ -393,28 +414,38 @@
         c1, c2, c3 = (at[axis] for axis in order)
         buf[c3, c2, c1] = piece
 
+    around = [(o1, o2) for o2 in (2, 1, 3, 0) for o1 in (2, 1, 3, 0) if (o1, o2) != (0, 0)]
     plan = []
     for buf, (w, _, order) in zip(gathered, PIECES):
-        plan.append((buf, order, tuple(at[axis] for axis in order), slots(3), slots(3), slots(6)))
-    for o in (2, 1, 3):
-        for buf, order, (c1, c2, c3), s1, s2, s3 in plan:
+        plan.append((buf, order, tuple(at[axis] for axis in order), slots(16), slots(6)))
+    for o1, o2 in around:
+        for buf, order, (c1, c2, c3), s1, s3 in plan:
             mine = buf.at[c3, c2, c1]
-            send(mine, mine, s1 + o - 1, peer(order[0], o))
-    for buf, order, (c1, c2, c3), s1, s2, s3 in plan:
-        for o in (1, 3, 2):
-            arrived(buf.at[c3, c2, (c1 + 4 - o) % 4], s1 + o - 1)
-        mine = buf.at[c3, c2]
-        for o in (2, 1, 3):
-            send(mine, mine, s2 + o - 1, peer(order[1], o))
-    for buf, order, (c1, c2, c3), s1, s2, s3 in plan:
-        for o in (1, 3, 2):
-            arrived(buf.at[c3, (c2 + 4 - o) % 4], s2 + o - 1)
+            send(mine, mine, s1 + o2 * 4 + o1, beside(order, o1, o2))
+
+    kept = hidden * keep
+    for j in range(7):
+        f1[j] = kept[:, j * 128 : (j + 1) * 128]
+    f2[...] = jnp.zeros_like(f2)
+    for t in range(2):
+        for j in range(7):
+            f2[pl.ds(t * 7 + j, 8, stride=16), :] = f1[j, pl.ds(t, 8, stride=2), :]
+    fsend[...] = f2[...].reshape(8, 16, 128).astype(BF16)
+    f_slot = slots(8)
+    for r in range(1, 8):
+        c = (chip + r) % 8
+        send(fsend.at[c], frecv.at[chip], f_slot + chip, member(c * 2 + k))
+    frecv[chip] = fsend[chip]
+
+    for buf, order, (c1, c2, c3), s1, s3 in plan:
+        for o1, o2 in reversed(around):
+            arrived(buf.at[c3, (c2 + 4 - o2) % 4, (c1 + 4 - o1) % 4], s1 + o2 * 4 + o1)
 
     def half(buf, c3, h):
         return buf.at[c3, pl.ds(2 * h, 2)]
 
     for h, o in ((0, 1), (1, 3), (0, 3), (1, 1)):
-        for buf, order, (c1, c2, c3), s1, s2, s3 in plan:
+        for buf, order, (c1, c2, c3), s1, s3 in plan:
             mine = half(buf, c3, h)
             send(mine, mine, s3 + (0 if o == 1 else 2) + h, peer(order[2], o))
 
@@ -442,14 +473,14 @@
     arrived(wgate.at[1 - k], w_slot)
     arrived(wup.at[1 - k], w_slot + 1)
     multiply(0, y, 0, 384)
-    for buf, order, (c1, c2, c3), s1, s2, s3 in plan:
+    for buf, order, (c1, c2, c3), s1, s3 in plan:
         for c, h, n, o in (((c3 + 3) % 4, 0, 0, 1), ((c3 + 1) % 4, 1, 3, 3)):
             view = half(buf, c, h)
             arrived(view, s3 + n)
             send(view, view, s3 + 4 + h, peer(order[2], o))
 
     def rest(n, last):
-        buf, order, (c1, c2, c3), s1, s2, s3 = plan[n]
+        buf, order, (c1, c2, c3), s1, s3 = plan[n]
         if last:
             arrived(half(buf, (c3 + 2) % 4, 0), s3 + 4)
             arrived(half(buf, (c3 + 2) % 4, 1), s3 + 5)
@@ -486,28 +517,39 @@
     expert = (p * 16 + s) // 8
     gate = jnp.sum(jnp.where(lane == expert, chosen, 0.0), axis=1, keepdims=True)
     gate = gate / jnp.sum(chosen, axis=1, keepdims=True) * route_scale
+    gate = gate * column_sum(lane == 65) * 0.125
     act = [jax.nn.silu(g * scale) * (u * scale) * gate for g, u in parts]
     act = jnp.concatenate(act, axis=1).astype(BF16)
+    to_row = lax.broadcasted_iota(jnp.int32, (128, 128), 0)
+    from_row = ((to_row >> 3) & 7) * 16 + (to_row & 7) * 2 + (to_row >> 6)
+    act = mm((from_row == lane).astype(BF16), act).astype(BF16)
 
     loads[7].wait()
     arrived(wdown.at[pl.ds(pl.multiple_of(256 - k * 256, 256), 256)], w_slot + 2)
     partial = (pa, pb, pc)
-    for yy in range(4):
-        for zz in range(2):
-            part = mm(act, wdown[:, pl.ds((yy * 2 + zz) * COLS, COLS)]).astype(BF16)
-            start = 0
-            for buf, (_, w, order) in zip(partial, PIECES):
-                for hh in range(2):
-                    for xx in range(4):
-                        at_block = {"x": xx, "y": yy, "z": hh * 2 + zz}
-                        c1, c2, c3 = (at_block[axis] for axis in order)
-                        first = (hh * 4 + xx) * 16
-                        buf[c3, c2, c1] = part[first : first + 16, start : start + w]
-                start += w
+
+    def project(n):
+        w, order = PIECES[n][1:]
+        start = sum(other_piece[1] for other_piece in PIECES[:n])
+        for c in range(8):
+            part = mm(act, wdown[:, pl.ds(c * COLS + start, w)])
+            for t in range(2):
+                for j in range(w // 128):
+                    block = part[t * 64 : t * 64 + 64, j * 128 : (j + 1) * 128]
+                    stage[start // 128 + j, pl.ds(2 * c + t, 64, stride=16), :] = block
+        for hh in range(2):
+            for xx in range(4):
+                for r in range(8):
+                    at_block = {"x": xx, "y": r // 2, "z": hh * 2 + r % 2}
+                    c1, c2, c3 = (at_block[axis] for axis in order)
+                    rows = pl.ds(((hh * 4 + xx) * 8 + r) * 16, 16)
+                    tiles = [stage[start // 128 + j, rows, :] for j in range(w // 128)]
+                    partial[n][c3, c2, c1] = jnp.concatenate(tiles, axis=1).astype(BF16)
+
     plan = []
     for n, (_, w, order) in enumerate(PIECES):
-        bufs = (partial[n], (r1a, r1b, r1c)[n], (r2a, r2b, r2c)[n], (r3a, r3b, r3c)[n])
-        plan.append((bufs, order, tuple(at[axis] for axis in order), slots(6), slots(3), slots(3)))
+        bufs = (partial[n], (r1a, r1b, r1c)[n], (r2a, r2b, r2c)[n])
+        plan.append((bufs, order, tuple(at[axis] for axis in order), slots(6), slots(16)))
 
     def add_to(ref, *terms):
         total = ref[...].astype(F32)
@@ -515,52 +557,50 @@
             total = total + term[...].astype(F32)
         ref[...] = total.astype(BF16)
 
-    for n, (step, h, o) in enumerate(((2, 0, 1), (2, 1, 3), (1, 1, 1), (3, 0, 3))):
-        for (part, r1, r2, r3), order, (c1, c2, c3), s1, s2, s3 in plan:
-            send(half(part, (c3 + step) % 4, h), r1.at[n], s1 + n, peer(order[2], o))
+    def pass_on(piece, step):
+        (part, r1, r2), order, (c1, c2, c3), s1, s2 = plan[piece]
+        for n, (to, h, o) in enumerate(((2, 0, 1), (2, 1, 3), (1, 1, 1), (3, 0, 3))):
+            if to == step:
+                send(half(part, (c3 + step) % 4, h), r1.at[n], s1 + n, peer(order[2], o))
+
+    for n in range(3):
+        project(n)
+        for step in (2, 1, 3):
+            pass_on(n, step)
     for n, (step, h, o) in enumerate(((1, 0, 1), (3, 1, 3))):
-        for (part, r1, r2, r3), order, (c1, c2, c3), s1, s2, s3 in plan:
+        for (part, r1, r2), order, (c1, c2, c3), s1, s2 in plan:
             view = half(part, (c3 + step) % 4, h)
             arrived(r1.at[n], s1 + n)
             add_to(view, r1.at[n])
             send(view, r1.at[n + 4], s1 + n + 4, peer(order[2], o))
-    for (part, r1, r2, r3), order, (c1, c2, c3), s1, s2, s3 in plan:
+    for (part, r1, r2), order, (c1, c2, c3), s1, s2 in plan:
         for n in (2, 3, 4, 5):
             arrived(r1.at[n], s1 + n)
         add_to(half(part, c3, 0), r1.at[3], r1.at[4])
         add_to(half(part, c3, 1), r1.at[2], r1.at[5])
-        for o in (2, 1, 3):
-            send(part.at[c3, (c2 + o) % 4], r2.at[o - 1], s2 + o - 1, peer(order[1], o))
-    for (part, r1, r2, r3), order, (c1, c2, c3), s1, s2, s3 in plan:
-        for o in (1, 2, 3):
-            arrived(r2.at[o - 1], s2 + o - 1)
-        add_to(part.at[c3, c2], r2.at[0], r2.at[1], r2.at[2])
-        for o in (2, 1, 3):
-            send(part.at[c3, c2, (c1 + o) % 4], r3.at[o - 1], s3 + o - 1, peer(order[0], o))
-    sums = []
-    for (part, r1, r2, r3), order, (c1, c2, c3), s1, s2, s3 in plan:
-        for o in (1, 2, 3):
-            arrived(r3.at[o - 1], s3 + o - 1)
-        sums.append(part[c3, c2, c1].astype(F32) + jnp.sum(r3[...].astype(F32), axis=0))
-    final = (jnp.concatenate(sums, axis=1) + hbuf[...]) * keep
-    for j in range(7):
-        f1[j] = final[:, j * 128 : (j + 1) * 128]
-
-    f2[...] = jnp.zeros_like(f2)
-    for t in range(2):
-        for j in range(7):
-            f2[pl.ds(t * 7 + j, 8, stride=16), :] = f1[j, pl.ds(t, 8, stride=2), :]
-    fsend[...] = f2[...].reshape(8, 16, 128).astype(BF16)
-    f_slot = slots(8)
-    for r in range(1, 8):
-        c = (chip + r) % 8
-        send(fsend.at[c], frecv.at[chip], f_slot + chip, member(c * 2 + k))
-    frecv[chip] = fsend[chip]
+        for o1, o2 in around:
+            block = part.at[c3, (c2 + o2) % 4, (c1 + o1) % 4]
+            send(block, r2.at[o2 * 4 + o1], s2 + o2 * 4 + o1, beside(order, o1, o2))
+
     for r in range(1, 8):
         c = (chip + r) % 8
         arrived(frecv.at[c], f_slot + c)
     f2[...] = frecv[...].reshape(128, 128).astype(F32)
-    rows = [f2[pl.ds(c * 16 + j, 2, stride=7), :] for c in range(8) for j in range(7)]
+
+    sums = []
+    for (part, r1, r2), order, (c1, c2, c3), s1, s2 in plan:
+        for o1, o2 in reversed(around):
+            arrived(r2.at[o2 * 4 + o1], s2 + o2 * 4 + o1)
+        got = r2[pl.ds(1, 15)].astype(F32)
+        sums.append(part[c3, c2, c1].astype(F32) + jnp.sum(got, axis=0))
+    final = jnp.concatenate(sums, axis=1)
+    for j in range(7):
+        f1[j] = final[:, j * 128 : (j + 1) * 128]
+    rows = [
+        f1[j, pl.ds(2 * c, 2), :] + f2[pl.ds(c * 16 + j, 2, stride=7), :]
+        for c in range(8)
+        for j in range(7)
+    ]
     result[...] = jnp.concatenate(rows, axis=1).astype(BF16)
     links.finish()
 
@@ -587,7 +627,7 @@
     scratch = [
         pltpu.VMEM((2, 576, positions), BF16),
         pltpu.VMEM((16, 512, 128), BF16),
-        pltpu.VMEM((256, 7168), BF16),
+        pltpu.VMEM((512, 7168), BF16),
         pltpu.VMEM((2, 7168, 256), BF16),
         pltpu.VMEM((2, 7168, 256), BF16),
         pltpu.VMEM((512, 7168), BF16),
@@ -595,23 +635,23 @@
         pltpu.VMEM((16, 2, 16, 576), BF16),
         pltpu.VMEM((128, 576), BF16),
         pltpu.VMEM((5, 512, 128), F32),
-        pltpu.VMEM((8, 32, 384), BF16),
-        pltpu.VMEM((8, 32, 384), BF16),
-        pltpu.VMEM((16, 16, COLS + 128), BF16),
-        pltpu.VMEM((16, 16, COLS + 128), BF16),
-        pltpu.VMEM((16, COLS), F32),
+        pltpu.VMEM((4, 2, 16, 640), BF16),
+        pltpu.VMEM((8, 16, 640), BF16),
+        pltpu.VMEM((8, 16, COLS + 128), BF16),
+        pltpu.VMEM((8, 16, COLS + 128), BF16),
+        pltpu.VMEM((7, 1024, 128), F32),
     ]
     scratch += [pltpu.VMEM((4, 4, 4, 16, w), BF16) for w, _, _ in PIECES]
     scratch += [pltpu.VMEM((4, 4, 4, 16, w), BF16) for _, w, _ in PIECES]
     scratch += [pltpu.VMEM((6, 2, 4, 16, w), BF16) for _, w, _ in PIECES]
-    scratch += [pltpu.VMEM((3, 4, 16, w), BF16) for _, w, _ in PIECES]
-    scratch += [pltpu.VMEM((3, 16, w), BF16) for _, w, _ in PIECES]
+    scratch += [pltpu.VMEM((16, 16, w), BF16) for _, w, _ in PIECES]
     scratch += [
         pltpu.VMEM((7, 16, 128), F32),
         pltpu.VMEM((128, 128), F32),
         pltpu.VMEM((8, 16, 128), BF16),
         pltpu.VMEM((8, 16, 128), BF16),
         pltpu.VMEM((56, 128), F32),
+        pltpu.VMEM((2, 16, 7296), BF16),
         pltpu.SemaphoreType.DMA((9,)),
         pltpu.SemaphoreType.DMA((192,)),
         pltpu.SemaphoreType.DMA((192,)),

time: 85.2 us -> 78.9 us (0.926)
  Pallas kernels: 83 us -> 76.7 us
    pallas_call x1, Pallas kernels: 83 us -> 76.7 us  [local(): pl.pallas_call(kernel, out_shape=jax.ShapeDtypeStruct((2, 7168), BF16), i...]
where the time goes in v3:
time: 78.9 us; the launch traced here: 78.7 us
  Pallas kernels  76.7 us (97%)
  local copies, waits for them, and re-layouts  1.38 us (2%)
    pallas_call x1, Pallas kernels, local(): pl.pallas_call(kernel, out_shape=jax.ShapeDtypeStruct((2, 7168), BF16), i...  76.7 us

profile of v3, /device:TPU:0, one launch (start us, length us, event | category | flops | bytes accessed | tf_op | source)
XLA Modules:
  0.0 78.7 jit_solution(4242595776522903507)
XLA Ops:
  0.7 76.7 %layer.1 = bf16[2,7168]{1,0:T(2,128)(2,1)} custom-call(bf16[2,32,576]{2,1,0:T(8,128)(2,1)} %q_in.1, bf16[576,2048]{1,0:T(8,128)(2,1)} %bitcast.11, bf16[32,512,128]{2,1,0:T(8,128)(2,1)} %uv_in.1, bf16[256,7168]{1,0:T(8,128)(2,1)} %out_in.1, bf16[16,7168]{1,0:T(8,128)(2,1)} %bitcast.12, bf16[7168,256]{1,0:T(8,128)(2,1)} %bitcast.8, ...), custom_call_target="tpu_custom_call" | custom-call | tf_op jit(solution)/shard_map/layer/pallas_call | solution.py:659
  77.3 1.4 %copy.17 = bf16[2,7168]{1,0:T(2,128)(2,1)} copy(bf16[2,7168]{1,0:T(2,128)(2,1)} %layer.1) | data formatting | bytes 57344

commit v4 on v3

--- a/solution.py
+++ b/solution.py
@@ -105,6 +105,9 @@
     r2a,
     r2b,
     r2c,
+    ba,
+    bb,
+    bc,
     f1,
     f2,
     fsend,
@@ -441,8 +444,8 @@
         for o1, o2 in reversed(around):
             arrived(buf.at[c3, (c2 + 4 - o2) % 4, (c1 + 4 - o1) % 4], s1 + o2 * 4 + o1)
 
-    def half(buf, c3, h):
-        return buf.at[c3, pl.ds(2 * h, 2)]
+    def half(buf, c3, h, size=2):
+        return buf.at[c3, pl.ds(size * h, size)]
 
     for h, o in ((0, 1), (1, 3), (0, 3), (1, 1)):
         for buf, order, (c1, c2, c3), s1, s3 in plan:
@@ -520,31 +523,22 @@
     gate = gate * column_sum(lane == 65) * 0.125
     act = [jax.nn.silu(g * scale) * (u * scale) * gate for g, u in parts]
     act = jnp.concatenate(act, axis=1).astype(BF16)
-    to_row = lax.broadcasted_iota(jnp.int32, (128, 128), 0)
-    from_row = ((to_row >> 3) & 7) * 16 + (to_row & 7) * 2 + (to_row >> 6)
-    act = mm((from_row == lane).astype(BF16), act).astype(BF16)
-
     loads[7].wait()
     arrived(wdown.at[pl.ds(pl.multiple_of(256 - k * 256, 256), 256)], w_slot + 2)
     partial = (pa, pb, pc)
+    to_row = lax.broadcasted_iota(jnp.int32, (128, 128), 0)
 
     def project(n):
         w, order = PIECES[n][1:]
+        owner = {axis: (to_row >> shift) & 3 for axis, shift in zip(order, (0, 2, 5))}
+        prompt_row = ((owner["z"] >> 1) * 4 + owner["x"]) * 16
+        from_row = prompt_row + (owner["y"] * 2 + (owner["z"] & 1)) * 2 + ((to_row >> 4) & 1)
+        rows = mm((from_row == lane).astype(BF16), act).astype(BF16)
         start = sum(other_piece[1] for other_piece in PIECES[:n])
         for c in range(8):
-            part = mm(act, wdown[:, pl.ds(c * COLS + start, w)])
-            for t in range(2):
-                for j in range(w // 128):
-                    block = part[t * 64 : t * 64 + 64, j * 128 : (j + 1) * 128]
-                    stage[start // 128 + j, pl.ds(2 * c + t, 64, stride=16), :] = block
-        for hh in range(2):
-            for xx in range(4):
-                for r in range(8):
-                    at_block = {"x": xx, "y": r // 2, "z": hh * 2 + r % 2}
-                    c1, c2, c3 = (at_block[axis] for axis in order)
-                    rows = pl.ds(((hh * 4 + xx) * 8 + r) * 16, 16)
-                    tiles = [stage[start // 128 + j, rows, :] for j in range(w // 128)]
-                    partial[n][c3, c2, c1] = jnp.concatenate(tiles, axis=1).astype(BF16)
+            part = mm(rows, wdown[:, pl.ds(c * COLS + start, w)]).astype(BF16)
+            for chunk in range(4):
+                partial[n][chunk, c] = part[chunk * 32 : chunk * 32 + 32]
 
     plan = []
     for n, (_, w, order) in enumerate(PIECES):
@@ -557,11 +551,13 @@
             total = total + term[...].astype(F32)
         ref[...] = total.astype(BF16)
 
+    blocks = (ba, bb, bc)
+
     def pass_on(piece, step):
         (part, r1, r2), order, (c1, c2, c3), s1, s2 = plan[piece]
         for n, (to, h, o) in enumerate(((2, 0, 1), (2, 1, 3), (1, 1, 1), (3, 0, 3))):
             if to == step:
-                send(half(part, (c3 + step) % 4, h), r1.at[n], s1 + n, peer(order[2], o))
+                send(half(part, (c3 + step) % 4, h, 4), r1.at[n], s1 + n, peer(order[2], o))
 
     for n in range(3):
         project(n)
@@ -569,17 +565,27 @@
             pass_on(n, step)
     for n, (step, h, o) in enumerate(((1, 0, 1), (3, 1, 3))):
         for (part, r1, r2), order, (c1, c2, c3), s1, s2 in plan:
-            view = half(part, (c3 + step) % 4, h)
+            view = half(part, (c3 + step) % 4, h, 4)
             arrived(r1.at[n], s1 + n)
             add_to(view, r1.at[n])
             send(view, r1.at[n + 4], s1 + n + 4, peer(order[2], o))
-    for (part, r1, r2), order, (c1, c2, c3), s1, s2 in plan:
+    for piece, ((part, r1, r2), order, (c1, c2, c3), s1, s2) in enumerate(plan):
         for n in (2, 3, 4, 5):
             arrived(r1.at[n], s1 + n)
-        add_to(half(part, c3, 0), r1.at[3], r1.at[4])
-        add_to(half(part, c3, 1), r1.at[2], r1.at[5])
+        tiles = PIECES[piece][1] // 128
+        for h, (one, two) in enumerate(((3, 4), (2, 5))):
+            for i in range(4):
+                c = h * 4 + i
+                chunk = part[c3, c].astype(F32) + r1[one, i].astype(F32) + r1[two, i].astype(F32)
+                for t in range(2):
+                    for j in range(tiles):
+                        stage[j, pl.ds(2 * c + t, 16, stride=16), :] = chunk[
+                            t * 16 : t * 16 + 16, j * 128 : (j + 1) * 128
+                        ]
+        whole = jnp.concatenate([stage[j] for j in range(tiles)], axis=1)
+        blocks[piece][...] = whole.astype(BF16).reshape(4, 4, 16, tiles * 128)
         for o1, o2 in around:
-            block = part.at[c3, (c2 + o2) % 4, (c1 + o1) % 4]
+            block = blocks[piece].at[(c2 + o2) % 4, (c1 + o1) % 4]
             send(block, r2.at[o2 * 4 + o1], s2 + o2 * 4 + o1, beside(order, o1, o2))
 
     for r in range(1, 8):
@@ -588,11 +594,11 @@
     f2[...] = frecv[...].reshape(128, 128).astype(F32)
 
     sums = []
-    for (part, r1, r2), order, (c1, c2, c3), s1, s2 in plan:
+    for block, ((part, r1, r2), order, (c1, c2, c3), s1, s2) in zip(blocks, plan):
         for o1, o2 in reversed(around):
             arrived(r2.at[o2 * 4 + o1], s2 + o2 * 4 + o1)
         got = r2[pl.ds(1, 15)].astype(F32)
-        sums.append(part[c3, c2, c1].astype(F32) + jnp.sum(got, axis=0))
+        sums.append(block[c2, c1].astype(F32) + jnp.sum(got, axis=0))
     final = jnp.concatenate(sums, axis=1)
     for j in range(7):
         f1[j] = final[:, j * 128 : (j + 1) * 128]
@@ -639,12 +645,13 @@
         pltpu.VMEM((8, 16, 640), BF16),
         pltpu.VMEM((8, 16, COLS + 128), BF16),
         pltpu.VMEM((8, 16, COLS + 128), BF16),
-        pltpu.VMEM((7, 1024, 128), F32),
+        pltpu.VMEM((3, 256, 128), F32),
     ]
     scratch += [pltpu.VMEM((4, 4, 4, 16, w), BF16) for w, _, _ in PIECES]
-    scratch += [pltpu.VMEM((4, 4, 4, 16, w), BF16) for _, w, _ in PIECES]
-    scratch += [pltpu.VMEM((6, 2, 4, 16, w), BF16) for _, w, _ in PIECES]
+    scratch += [pltpu.VMEM((4, 8, 32, w), BF16) for _, w, _ in PIECES]
+    scratch += [pltpu.VMEM((6, 4, 32, w), BF16) for _, w, _ in PIECES]
     scratch += [pltpu.VMEM((16, 16, w), BF16) for _, w, _ in PIECES]
+    scratch += [pltpu.VMEM((4, 4, 16, w), BF16) for _, w, _ in PIECES]
     scratch += [
         pltpu.VMEM((7, 16, 128), F32),
         pltpu.VMEM((128, 128), F32),

time: 78.9 us -> 78.2 us (level)
  Pallas kernels: 76.7 us -> 75.9 us
where the time goes in v4:
time: 78.2 us; the launch traced here: 77.9 us
  Pallas kernels  75.9 us (97%)
  local copies, waits for them, and re-layouts  1.38 us (2%)
    pallas_call x1, Pallas kernels, local(): pl.pallas_call(kernel, out_shape=jax.ShapeDtypeStruct((2, 7168), BF16), i...  75.9 us

profile of v4, /device:TPU:0, one launch (start us, length us, event | category | flops | bytes accessed | tf_op | source)
XLA Modules:
  0.0 77.9 jit_solution(1718244335940004104)
XLA Ops:
  0.7 75.9 %layer.1 = bf16[2,7168]{1,0:T(2,128)(2,1)} custom-call(bf16[2,32,576]{2,1,0:T(8,128)(2,1)} %q_in.1, bf16[576,2048]{1,0:T(8,128)(2,1)} %bitcast.11, bf16[32,512,128]{2,1,0:T(8,128)(2,1)} %uv_in.1, bf16[256,7168]{1,0:T(8,128)(2,1)} %out_in.1, bf16[16,7168]{1,0:T(8,128)(2,1)} %bitcast.12, bf16[7168,256]{1,0:T(8,128)(2,1)} %bitcast.8, ...), custom_call_target="tpu_custom_call" | custom-call | tf_op jit(solution)/shard_map/layer/pallas_call | solution.py:666
  76.6 1.4 %copy.17 = bf16[2,7168]{1,0:T(2,128)(2,1)} copy(bf16[2,7168]{1,0:T(2,128)(2,1)} %layer.1) | data formatting | bytes 57344

commit v5 on v4

--- a/solution.py
+++ b/solution.py
@@ -146,6 +146,20 @@
     other = (p, y * 4 + zl * 2 + (1 - k))
     across = (p, y * 4 + (1 - zl) * 2 + k)
 
+    barrier = pltpu.get_barrier_semaphore()
+    partners = [member((s + r) % 16) for r in range(1, 16)]
+    planes = [(dx, dy, dz) for dx in range(4) for dy in range(4) for dz in range(4) if 0 in (dx, dy, dz)]
+    for dx, dy, dz in planes:
+        if dx:
+            partners.append(device((x + dx) % 4, (y + dy) % 4, (z + dz) % 4, k))
+        elif dz in (1, 3):
+            if dz == 1:
+                partners.append(device(x, (y + dy) % 4, (1 - zh) * 2, k))
+            else:
+                partners.append(device(x, (y + dy) % 4, (1 - zh) * 2 + 1, k))
+    for there in partners:
+        pl.semaphore_signal(barrier, inc=1, device_id=there, device_id_type=MESH)
+
     first_column = pl.multiple_of(chip * COLS, 128)
     own_heads = pl.ds(pl.multiple_of(k * 16, 16), 16)
     own_units = pl.ds(pl.multiple_of(k * 256, 256), 256)
@@ -167,19 +181,6 @@
     for n in (0, 1, 2):
         loads[n].start()
 
-    barrier = pltpu.get_barrier_semaphore()
-    partners = [member((s + r) % 16) for r in range(1, 16)]
-    planes = [(dx, dy, dz) for dx in range(4) for dy in range(4) for dz in range(4) if 0 in (dx, dy, dz)]
-    for dx, dy, dz in planes:
-        if dx:
-            partners.append(device((x + dx) % 4, (y + dy) % 4, (z + dz) % 4, k))
-        elif dz in (1, 3):
-            if dz == 1:
-                partners.append(device(x, (y + dy) % 4, (1 - zh) * 2, k))
-            else:
-                partners.append(device(x, (y + dy) % 4, (1 - zh) * 2 + 1, k))
-    for there in partners:
-        pl.semaphore_signal(barrier, inc=1, device_id=there, device_id_type=MESH)
     pl.semaphore_wait(barrier, len(partners))
 
     links = Links(send_sem, recv_sem, other)
@@ -278,15 +279,18 @@
     loads[1].wait()
     arrived(kn.at[pl.ds(pl.multiple_of(16 - k * 16, 16), 16)], k_slot + 1)
     arrived(kc.at[1 - k], k_slot)
-    for n in (3, 4, 5, 6, 7):
+    for n in (3, 4):
         loads[n].start()
     w_slot = slots(4)
     send(out_in, wout.at[own_units], w_slot + 3, other)
+    attend(y, (y + 1) % 4, True)
+    attend((y + 3) % 4, (y + 2) % 4, False)
+
+    for n in (5, 6, 7):
+        loads[n].start()
     send(gate_in, wgate.at[k], w_slot, other)
     send(up_in, wup.at[k], w_slot + 1, other)
     send(down_in, wdown.at[own_units], w_slot + 2, other)
-    attend(y, (y + 1) % 4, True)
-    attend((y + 3) % 4, (y + 2) % 4, False)
 
     targets = assign[...]
     places = ((targets >> 1) & 1) * 16 + (targets >> 2) * 2 + (targets & 1)
@@ -494,12 +498,6 @@
     rest(0, False)
     multiply(0, (y + 3) % 4, 0, 384)
     multiply(0, (y + 1) % 4, 0, 384)
-    rest(0, True)
-    multiply(0, (y + 2) % 4, 0, 384)
-    rest(1, False)
-    rest(1, True)
-    for yy in range(4):
-        multiply(1, yy, 384, 384)
     rest(2, False)
     rest(2, True)
     note = jnp.zeros((128, 128), F32)
@@ -521,6 +519,12 @@
     gate = jnp.sum(jnp.where(lane == expert, chosen, 0.0), axis=1, keepdims=True)
     gate = gate / jnp.sum(chosen, axis=1, keepdims=True) * route_scale
     gate = gate * column_sum(lane == 65) * 0.125
+    rest(0, True)
+    multiply(0, (y + 2) % 4, 0, 384)
+    rest(1, False)
+    rest(1, True)
+    for yy in range(4):
+        multiply(1, yy, 384, 384)
     act = [jax.nn.silu(g * scale) * (u * scale) * gate for g, u in parts]
     act = jnp.concatenate(act, axis=1).astype(BF16)
     loads[7].wait()
@@ -569,7 +573,8 @@
             arrived(r1.at[n], s1 + n)
             add_to(view, r1.at[n])
             send(view, r1.at[n + 4], s1 + n + 4, peer(order[2], o))
-    for piece, ((part, r1, r2), order, (c1, c2, c3), s1, s2) in enumerate(plan):
+    for piece in (2, 1, 0):
+        (part, r1, r2), order, (c1, c2, c3), s1, s2 = plan[piece]
         for n in (2, 3, 4, 5):
             arrived(r1.at[n], s1 + n)
         tiles = PIECES[piece][1] // 128

time: 78.2 us -> 78.2 us (level)
  no operation moved by 1% of the time
where the time goes in v5:
time: 78.2 us; the launch traced here: 78 us
  Pallas kernels  76 us (97%)
  local copies, waits for them, and re-layouts  1.38 us (2%)
    pallas_call x1, Pallas kernels, local(): pl.pallas_call(kernel, out_shape=jax.ShapeDtypeStruct((2, 7168), BF16), i...  76 us

profile of v5, /device:TPU:0, one launch (start us, length us, event | category | flops | bytes accessed | tf_op | source)
XLA Modules:
  0.0 78.0 jit_solution(739306042553257159)
XLA Ops:
  0.7 76.0 %layer.1 = bf16[2,7168]{1,0:T(2,128)(2,1)} custom-call(bf16[2,32,576]{2,1,0:T(8,128)(2,1)} %q_in.1, bf16[576,2048]{1,0:T(8,128)(2,1)} %bitcast.11, bf16[32,512,128]{2,1,0:T(8,128)(2,1)} %uv_in.1, bf16[256,7168]{1,0:T(8,128)(2,1)} %out_in.1, bf16[16,7168]{1,0:T(8,128)(2,1)} %bitcast.12, bf16[7168,256]{1,0:T(8,128)(2,1)} %bitcast.8, ...), custom_call_target="tpu_custom_call" | custom-call | tf_op jit(solution)/shard_map/layer/pallas_call | solution.py:671
  76.6 1.4 %copy.17 = bf16[2,7168]{1,0:T(2,128)(2,1)} copy(bf16[2,7168]{1,0:T(2,128)(2,1)} %layer.1) | data formatting | bytes 57344
